TPU v7x, 32 devices: a whole 2x2x4 slice. The times are simulated.
32 devices in a mesh: tm: 4 (over z), dp: 8 (over y, x, core).
Axes of the slice: x: 2, y: 2, z: 4, core: 2. Of those that a mesh axis runs over, the one named last changes fastest.
Arguments:
- clip_video: bfloat16 [8, 8, 4, 16, 192], P('dp', 'tm'), may hold values from -6 to 6
- clip_ids: int32 [8, 8], P('dp'), may hold values from 0 to 3, never falling along the last dimension, each value on 1 to 4 neighbouring positions
- norm_gain: float32 [192], replicated, may hold values from 0.25 to 1.75
- conv_weight: bfloat16 [5184, 384], replicated, may hold values from -0.078125 to 0.078125
- out_cotangent: bfloat16 [8, 8, 4, 16, 384], P('dp', 'tm'), may hold values from -6 to 6
Outputs:
- conv_out: bfloat16 [8, 8, 4, 16, 384], P('dp', 'tm')
- grad_video: bfloat16 [8, 8, 4, 16, 192], P('dp', 'tm')
- grad_weight: float32 [5184, 384], P('tm', 'dp')
Inputs may be any that keep to these rules, and one draw needn't show every extreme that they name: `clip_ids`: within each group clip numbers never fall along the frames; each clip lasts 1 to 4 frames and one lasts exactly 4.
All inputs are finite; a program needn't handle non-finite values.
Results may differ from a plain program's by a relative error of at most 0.0049.
Values may be sent and summed in bfloat16 or wider, within the bound.
A program may use at most 64 MiB of HBM per device.

v0:
```python
import math

import jax
import jax.numpy as jnp
from jax import lax
from jax.sharding import PartitionSpec as P


def from_behind(block, axis, distance):
    devices = range(lax.axis_size(axis))
    route = [(i - distance, i) for i in devices if i - distance in devices]
    return lax.ppermute(block, axis, route)


def activate(video, norm_gain):
    values = video.astype(jnp.float32)
    mean_square = jnp.mean(values * values, axis=-1, keepdims=True)
    normed = values * lax.rsqrt(mean_square + 1e-06) * norm_gain
    return jax.nn.silu(normed)


def make_mask(clips, first_frame, count):
    padded_ids = jnp.concatenate([jnp.full((2,), -1, jnp.int32), clips])
    window = lax.dynamic_slice_in_dim(padded_ids, first_frame, count + 2)
    offsets = jnp.arange(count)[:, None] + jnp.arange(3)[None, :]
    current = window[jnp.arange(count) + 2][:, None]
    return (window[offsets] == current).astype(jnp.float32)


def extract(extended, tap_mask):
    frames = tap_mask.shape[0]
    height, width = (extended.shape[1], extended.shape[2])
    padded = jnp.pad(extended, ((0, 0), (1, 1), (1, 1), (0, 0)))
    taps = []
    for tap_t in range(3):
        weight_t = tap_mask[:, tap_t][:, None, None, None].astype(extended.dtype)
        for tap_h in range(3):
            for tap_w in range(3):
                taps.append(
                    padded[tap_t : tap_t + frames, tap_h : tap_h + height, tap_w : tap_w + width]
                    * weight_t
                )
    stacked = jnp.stack(taps, axis=3)
    return stacked.reshape(frames * height * width, -1)


def shards(clip_video, clip_ids, norm_gain, conv_weight, out_cotangent):
    video = clip_video[0]
    frames, height, width, channels = video.shape
    outputs = conv_weight.shape[1]
    activated = activate(video, norm_gain).astype(jnp.bfloat16)
    previous = from_behind(activated, "tm", 1)
    extended = jnp.concatenate([previous, activated])
    first_frame = lax.axis_index("tm") * frames
    tap_mask = make_mask(clip_ids[0], first_frame, frames)
    patches = extract(extended, tap_mask)
    conv_rows = jnp.dot(patches, conv_weight, preferred_element_type=jnp.float32).astype(
        jnp.bfloat16
    )
    cotangent_rows = out_cotangent[0].reshape(-1, outputs)
    patch_grad = jnp.dot(cotangent_rows, conv_weight.T, preferred_element_type=jnp.float32)
    unused, pull_patch = jax.vjp(
        lambda field: extract(field, tap_mask), extended.astype(jnp.float32)
    )
    extended_grad = pull_patch(patch_grad)[0]
    returned = from_behind(extended_grad[:2], "tm", -1)
    own_grad = extended_grad[2:] + returned
    unused, pull_norm = jax.vjp(lambda field: activate(field, norm_gain), video.astype(jnp.float32))
    video_grad = pull_norm(own_grad)[0].astype(jnp.bfloat16)
    chain_len = lax.axis_size("tm")
    scale = 1.0 / math.sqrt(lax.axis_size("dp") * chain_len * frames * height * width)
    kernel_rows = patches.shape[1]
    slab_rows = kernel_rows // chain_len
    slab_start = lax.axis_index("tm") * slab_rows

    def slab_term(block_ext, block_cot, block_mask):
        block_patches = extract(block_ext, block_mask)
        slab_part = lax.dynamic_slice_in_dim(block_patches, slab_start, slab_rows, 1)
        cot_rows = block_cot.reshape(-1, outputs)
        return jnp.dot(slab_part.T, cot_rows, preferred_element_type=jnp.float32)

    start_slab = jnp.zeros((slab_rows, outputs), jnp.float32)

    def add_block(total, block):
        block_ext, block_cot, block_mask = block
        return (total + slab_term(block_ext, block_cot, block_mask), None)

    total = start_slab
    total, unused_out = lax.scan(
        add_block,
        total,
        (
            lax.all_gather(extended[None], "tm", axis=0, tiled=True),
            lax.all_gather(out_cotangent, "tm", axis=0, tiled=True),
            lax.all_gather(tap_mask.astype(jnp.bfloat16)[None], "tm", axis=0, tiled=True),
        ),
    )
    grad_weight = lax.psum_scatter(total * scale, "dp", scatter_dimension=1, tiled=True)
    conv_out = conv_rows.reshape(1, frames, height, width, outputs)
    return (conv_out, video_grad[None], grad_weight)


def solution(mesh):
    in_specs = (
        P("dp", "tm", None, None, None),
        P("dp", None),
        P(),
        P(),
        P("dp", "tm", None, None, None),
    )
    out_specs = (P("dp", "tm", None, None, None), P("dp", "tm", None, None, None), P("tm", "dp"))
    return jax.shard_map(shards, mesh=mesh, in_specs=in_specs, out_specs=out_specs, check_vma=False)
```

profile of v0, /device:TPU:0, one launch (start us, length us, event | category | flops | bytes accessed | tf_op | source)
XLA Modules:
  0.0 239.3 jit_solution(6697437037199435615)
XLA Ops:
  9.7 4.1 %fusion.134 = f32[2,4,16,27,192]{4,2,3,1,0:T(8,128)S(1)} fusion(bf16[27,192,384,1,1]{2,1,0,4,3:T(8,128)(2,1)} %bitcast.540, bf16[1,2,4,16,384]{4,3,2,1,0:T(8,128)(2,1)} %param.11), kind=kOutput, calls=%fused_computation.232 | convolution fusion | flops 509607936 | bytes 6733824 | tf_op jit(solution)/shard_map/dot_general | solution.py:61
  16.7 13.6 %all_gather.10 = bf16[4,2,3]{2,1,0:T(2,128)(2,1)S(1)} all-gather(bf16[1,2,3]{2,1,0:T(2,128)(2,1)S(1)} %fusion.216), channel_id=1, replica_groups=mesh['tm'=4,'dp'=8] {'tm'}, dimensions={0}, use_global_device_ids=true | all-gather | bytes 60 | tf_op jit(solution)/shard_map/all_gather | solution.py:95
  30.4 14.4 %all_gather.11 = bf16[4,2,4,16,384]{4,3,2,1,0:T(8,128)(2,1)S(1)} all-gather(bf16[1,2,4,16,384]{4,3,2,1,0:T(8,128)(2,1)S(1)} %copy-done.1), channel_id=1, replica_groups=mesh['tm'=4,'dp'=8] {'tm'}, dimensions={0}, use_global_device_ids=true | all-gather | bytes 491520 | tf_op jit(solution)/shard_map/all_gather | solution.py:94
  47.0 1.7 collective-permute-done
  48.7 16.2 %all-gather = bf16[16,4,16,192]{3,2,1,0:T(8,128)(2,1)S(1)} all-gather(bf16[4,4,16,192]{3,2,1,0:T(8,128)(2,1)S(1)} %pad_maximum_fusion), channel_id=2, replica_groups=mesh['tm'=4,'dp'=8] {'tm'}, dimensions={0}, use_global_device_ids=true | all-gather | bytes 491520 | tf_op jit(solution)/shard_map/all_gather | solution.py:93
  75.3 111.3 %while.13 = (s32[]{:T(128)}, f32[1296,384]{1,0:T(8,128)}, bf16[4,4,4,16,192]{4,3,2,1,0:T(8,128)(2,1)S(1)}, bf16[4,2,3]{2,1,0:T(2,128)(2,1)S(1)}, s32[]{:T(128)},...) while((s32[]{:T(128)}, f32[1296,384]{1,0:T(8,128)}, ...), condition=%wide.region_3.4_spmd.clone, body=%wide.region_2.3_spmd.clone.sunk | while | flops 131051520 | bytes 14420279 | solution.py:89
  94.4 2.5 %copy.182 = bf16[2,4,16,27,192]{4,3,2,1,0:T(8,128)(2,1)S(1)} copy(bf16[2,4,16,27,192]{4,2,1,0,3:T(8,128)(2,1)} %fusion.282) | data formatting | bytes 2654208 | tf_op jit(solution)/shard_map/while/body/eval_jaxpr/stack | solution.py:43
  96.9 2.8 %reshape.245 = bf16[128,5184]{1,0:T(8,128)(2,1)} reshape(bf16[2,4,16,27,192]{4,3,2,1,0:T(8,128)(2,1)S(1)} %copy.182) | data formatting | bytes 2654208 | tf_op jit(solution)/shard_map/while/body/eval_jaxpr/reshape | solution.py:44
  99.8 2.9 %convolution_add_fusion.2 = f32[1296,384]{1,0:T(8,128)} fusion(bf16[128,384]{1,0:T(8,128)(2,1)S(1)} %bitcast.541, f32[1296,384]{1,0:T(8,128)} %get-tuple-element.216, pred[]{:T(512)S(6)} %compare.33, bf16[128,5184]{1,0:T(8,128)(2,1)} %reshape.245, s32[]{:T(128)} %get-tuple-element.229), kind=kOutput, calls=%fused_computation.2.clone.1 | convolution fusion | flops 128397312 | bytes 4440577 | tf_op jit(solution)/shard_map/while/body/eval_jaxpr/dot_general | solution.py:80
  121.7 2.5 %copy.182 = bf16[2,4,16,27,192]{4,3,2,1,0:T(8,128)(2,1)S(1)} copy(bf16[2,4,16,27,192]{4,2,1,0,3:T(8,128)(2,1)} %fusion.282) | data formatting | bytes 2654208 | tf_op jit(solution)/shard_map/while/body/eval_jaxpr/stack | solution.py:43
  124.2 2.8 %reshape.245 = bf16[128,5184]{1,0:T(8,128)(2,1)} reshape(bf16[2,4,16,27,192]{4,3,2,1,0:T(8,128)(2,1)S(1)} %copy.182) | data formatting | bytes 2654208 | tf_op jit(solution)/shard_map/while/body/eval_jaxpr/reshape | solution.py:44
  127.1 3.6 %convolution_add_fusion.2 = f32[1296,384]{1,0:T(8,128)} fusion(bf16[128,384]{1,0:T(8,128)(2,1)S(1)} %bitcast.541, f32[1296,384]{1,0:T(8,128)} %get-tuple-element.216, pred[]{:T(512)S(6)} %compare.33, bf16[128,5184]{1,0:T(8,128)(2,1)} %reshape.245, s32[]{:T(128)} %get-tuple-element.229), kind=kOutput, calls=%fused_computation.2.clone.1 | convolution fusion | flops 128397312 | bytes 4440577 | tf_op jit(solution)/shard_map/while/body/eval_jaxpr/dot_general | solution.py:80
  149.7 2.5 %copy.182 = bf16[2,4,16,27,192]{4,3,2,1,0:T(8,128)(2,1)S(1)} copy(bf16[2,4,16,27,192]{4,2,1,0,3:T(8,128)(2,1)} %fusion.282) | data formatting | bytes 2654208 | tf_op jit(solution)/shard_map/while/body/eval_jaxpr/stack | solution.py:43
  152.2 2.8 %reshape.245 = bf16[128,5184]{1,0:T(8,128)(2,1)} reshape(bf16[2,4,16,27,192]{4,3,2,1,0:T(8,128)(2,1)S(1)} %copy.182) | data formatting | bytes 2654208 | tf_op jit(solution)/shard_map/while/body/eval_jaxpr/reshape | solution.py:44
  155.1 3.6 %convolution_add_fusion.2 = f32[1296,384]{1,0:T(8,128)} fusion(bf16[128,384]{1,0:T(8,128)(2,1)S(1)} %bitcast.541, f32[1296,384]{1,0:T(8,128)} %get-tuple-element.216, pred[]{:T(512)S(6)} %compare.33, bf16[128,5184]{1,0:T(8,128)(2,1)} %reshape.245, s32[]{:T(128)} %get-tuple-element.229), kind=kOutput, calls=%fused_computation.2.clone.1 | convolution fusion | flops 128397312 | bytes 4440577 | tf_op jit(solution)/shard_map/while/body/eval_jaxpr/dot_general | solution.py:80
  177.7 2.5 %copy.182 = bf16[2,4,16,27,192]{4,3,2,1,0:T(8,128)(2,1)S(1)} copy(bf16[2,4,16,27,192]{4,2,1,0,3:T(8,128)(2,1)} %fusion.282) | data formatting | bytes 2654208 | tf_op jit(solution)/shard_map/while/body/eval_jaxpr/stack | solution.py:43
  180.2 2.8 %reshape.245 = bf16[128,5184]{1,0:T(8,128)(2,1)} reshape(bf16[2,4,16,27,192]{4,3,2,1,0:T(8,128)(2,1)S(1)} %copy.182) | data formatting | bytes 2654208 | tf_op jit(solution)/shard_map/while/body/eval_jaxpr/reshape | solution.py:44
  183.1 3.6 %convolution_add_fusion.2 = f32[1296,384]{1,0:T(8,128)} fusion(bf16[128,384]{1,0:T(8,128)(2,1)S(1)} %bitcast.541, f32[1296,384]{1,0:T(8,128)} %get-tuple-element.216, pred[]{:T(512)S(6)} %compare.33, bf16[128,5184]{1,0:T(8,128)(2,1)} %reshape.245, s32[]{:T(128)} %get-tuple-element.229), kind=kOutput, calls=%fused_computation.2.clone.1 | convolution fusion | flops 128397312 | bytes 4440577 | tf_op jit(solution)/shard_map/while/body/eval_jaxpr/dot_general | solution.py:80
  186.7 1.7 broadcast_multiply_fusion
  188.4 2.0 copy.153
  198.7 2.6 %copy.123 = bf16[2,4,16,27,192]{4,3,2,1,0:T(8,128)(2,1)S(1)} copy(bf16[2,4,16,27,192]{4,2,1,0,3:T(8,128)(2,1)} %fusion.214) | data formatting | bytes 2654208 | tf_op jit(solution)/shard_map/stack | solution.py:43
  201.3 2.8 %reshape.209 = bf16[128,5184]{1,0:T(8,128)(2,1)} reshape(bf16[2,4,16,27,192]{4,3,2,1,0:T(8,128)(2,1)S(1)} %copy.123) | data formatting | bytes 2654208 | tf_op jit(solution)/shard_map/reshape | solution.py:44
  204.2 4.0 %convolution_convert_fusion = bf16[128,384]{1,0:T(8,128)(2,1)} fusion(bf16[128,5184]{1,0:T(8,128)(2,1)} %reshape.209, bf16[5184,384]{1,0:T(8,128)(2,1)} %param.10), kind=kOutput, calls=%fused_computation.141 | convolution fusion | flops 509657088 | bytes 5406720 | tf_op jit(solution)/shard_map/dot_general | solution.py:57
  208.2 24.2 %reduce-scatter.4.cloned.1.call-done = f32[48,1296]{1,0:T(8,128)} async-done(((f32[384,1296]{1,0:T(8,128)}), f32[48,1296]{1,0:T(8,128)}) %reduce-scatter.4.cloned.1.call-update) | async-done | bytes 248848
  (189 shorter events, 102.6 us)
Async XLA Ops:
  7.2 225.3 %reduce-scatter.4.cloned.1.call-start = ((), (), s32[]{:S(2)}) async-start(), calls=%async_computation.1 | async-start | bytes 2433024
  14.5 2.1 copy-start
  14.5 15.9 %copy-start.1 = (bf16[1,2,4,16,384]{4,3,2,1,0:T(8,128)(2,1)S(1)}, bf16[1,2,4,16,384]{4,3,2,1,0:T(8,128)(2,1)}, u32[]{:S(2)}) copy-start(bf16[1,2,4,16,384]{4,3,2,1,0:T(8,128)(2,1)} %param.11) | copy-start | bytes 294916
  14.5 30.2 %copy-start.2 = (f32[192]{0:T(256)S(1)}, f32[192]{0:T(256)}, u32[]{:S(2)}) copy-start(f32[192]{0:T(256)} %param.9) | copy-start | bytes 2308
  15.1 29.6 %collective-permute-start.1 = (f32[2,4,16,192]{3,2,1,0:T(8,128)S(1)}, f32[2,4,16,192]{3,2,1,0:T(8,128)S(1)}, u32[]{:S(2)}, u32[]{:S(2)}) collective-permute-start(f32[2,4,16,192]{3,2,1,0:T(8,128)S(1)} %slice.363), channel_id=1, source_target_pairs={{8,0},{16,8},{24,16},{9,1},{17,9},{25,17},{10,2},{18,10},{26,18},{... | collective-permute-start | bytes 294920 | tf_op jit(solution)/shard_map/ppermute | solution.py:12
  45.0 3.7 %collective-permute-start = (bf16[2,4,16,192]{3,2,1,0:T(8,128)(2,1)S(1)}, bf16[2,4,16,192]{3,2,1,0:T(8,128)(2,1)S(1)}, u32[]{:S(2)}, u32[]{:S(2)}) collective-permute-start(bf16[2,4,16,192]{3,2,1,0:T(8,128)(2,1)S(1)} %get-tuple-element.159), channel_id=1, source_target_pairs={{0,8},{8,16},{16,24},{1,9},{9,17},{17,25},{2,10},{10,18},{18,26},{... | collective-permute-start | bytes 147464 | tf_op jit(solution)/shard_map/ppermute | solution.py:12
Sparse Core Ops, SparseCore 0:
  190.5 41.9 reduce-scatter.3
where the time goes:
time: 240 us; the launch traced here: 239 us
  other arithmetic  98.1 us (41%)
  blocking collectives  44.2 us (18%)
  local copies, waits for them, and re-layouts  32.2 us (13%)
  waiting for transfers between devices  25.9 us (11%)
  matrix products  21.8 us (9%)
  between operations  14.2 us (6%)
  starting transfers between devices  2.62 us (1%)
    while x104, other arithmetic  72.4 us
    unnamed x2, waiting for transfers between devices  24.2 us
    unnamed x27, other arithmetic  18.1 us
    all_gather x1, blocking collectives, shards(): lax.all_gather(extended[None], 'tm', axis=0, tiled=True)  16.2 us
    all_gather x1, blocking collectives, shards(): lax.all_gather(out_cotangent, 'tm', axis=0, tiled=True)  14.4 us
    reshape x5, local copies, waits for them, and re-layouts, extract(): return stacked.reshape(frames * height * width, -1)  14.2 us
    dot_general x4, matrix products, slab_term(): return jnp.dot(slab_part.T, cot_rows, preferred_element_type=jnp.float32)  13.7 us
    all_gather x1, blocking collectives, shards(): lax.all_gather(tap_mask.astype(jnp.bfloat16)[None], 'tm', axis=0, tiled=T...  13.6 us
  transfers between devices with their start and end apart: 3, of which 2 were waited for; matrix products, arithmetic and copies ran while one was open for 8% of the time, Pallas kernels for 0%

commit v1 on v0

v1 whole, which is shorter than its diff:
```python
import functools
import math

import jax
import jax.numpy as jnp
from jax import lax
from jax.experimental import pallas as pl
from jax.experimental.pallas import tpu as pltpu
from jax.sharding import PartitionSpec as P

MESH = pl.DeviceIdType.MESH
F32 = jnp.float32
BF16 = jnp.bfloat16


def half_roll(x):
    return pltpu.roll(x, 64, axis=1)


def shifted(x, width, b):
    if b == 1:
        return x
    rows = x.shape[0]
    column = lax.broadcasted_iota(jnp.int32, x.shape, 0) % width
    if b == 0:
        return jnp.where(column == 0, 0.0, pltpu.roll(x, 1, axis=0))
    return jnp.where(column == width - 1, 0.0, pltpu.roll(x, rows - 1, axis=0))


def kernel(
    cfg, video_ref, ids_ref, gain_ref, w_hbm, cot_ref, conv_ref, vgrad_ref, gw_ref,
    w_ref, pay, ext, cext, mask, cot_t, d32, d16, r1, s16, s32, r2,
    w_sem, send_r, send_l, recv_r, recv_l, core_send, core_recv, chip_send, chip_recv,
):
    tm, dp, frames, height, width, cin, cout, slab, pairs, fused = cfg
    total = tm * frames
    rows = frames * height * width
    pixels = height * width
    chunks = cout // 128
    z = lax.axis_index("tm")
    j = lax.axis_index("dp")
    core = j % 2
    chip = j // 2
    chips = dp // 2
    per = cout // dp

    w_copy = pltpu.make_async_copy(w_hbm, w_ref, w_sem)
    w_copy.start()

    barrier = pltpu.get_barrier_semaphore()

    def greet(where):
        pl.semaphore_signal(barrier, inc=1, device_id=where, device_id_type=MESH)

    @pl.when(z > 0)
    def _():
        greet((z - 1, j))

    @pl.when(z < tm - 1)
    def _():
        greet((z + 1, j))

    if fused:
        greet((z, chip * 2 + 1 - core))
        for r in range(1, chips):
            greet((z, (chip + r) % chips * 2 + core))

    video = video_ref[...].astype(F32)
    gain = gain_ref[...]
    mean_square = jnp.sum(video * video, axis=1, keepdims=True) / cin
    inv = lax.rsqrt(mean_square + 1e-06)
    normed = video * inv * gain
    sig = jax.nn.sigmoid(normed)
    act = (normed * sig).astype(BF16).astype(F32)
    lane = lax.broadcasted_iota(jnp.int32, (rows, 128), 1)
    low = lane < 64
    first = act[:, :128]
    second = jnp.concatenate([act[:, 128:], jnp.zeros((rows, 64), F32)], axis=1)
    half = rows // 2
    for m in range(chunks):
        pay[z, m * rows : (m + 1) * rows, :] = cot_ref[:, m * 128 : (m + 1) * 128]
    pay[z, chunks * rows : (chunks + 1) * rows, :] = first.astype(BF16)
    pay[z, (chunks + 1) * rows :, :] = (second[:half] + half_roll(second[half:])).astype(BF16)

    peers = jnp.where(z > 0, 1, 0) + jnp.where(z < tm - 1, 1, 0)
    if fused:
        peers = peers + chips
    pl.semaphore_wait(barrier, peers)

    def to_right(step, shard):
        return pltpu.make_async_remote_copy(
            src_ref=pay.at[shard], dst_ref=pay.at[shard], send_sem=send_r.at[step],
            recv_sem=recv_r.at[step], device_id=(z + 1, j), device_id_type=MESH,
        )

    def to_left(step, shard):
        return pltpu.make_async_remote_copy(
            src_ref=pay.at[shard], dst_ref=pay.at[shard], send_sem=send_l.at[step],
            recv_sem=recv_l.at[step], device_id=(z - 1, j), device_id_type=MESH,
        )

    def start_step(step):
        @pl.when((z < tm - 1) & (z - step >= 0))
        def _():
            to_right(step, z - step).start()

        @pl.when((z > 0) & (z + step <= tm - 1))
        def _():
            to_left(step, z + step).start()

    start_step(0)

    ext[...] = jnp.zeros(ext.shape, BF16)
    cext[...] = jnp.zeros(cext.shape, BF16)
    mask[...] = jnp.zeros(mask.shape, BF16)
    for t in range(total):
        for k in range(3):
            if t - 2 + k >= 0:
                same = jnp.where(ids_ref[0, t - 2 + k] == ids_ref[0, t], 1.0, 0.0)
                mask[k, t] = jnp.full((pixels, 128), same, F32).astype(BF16)

    def blocks(x):
        return x.astype(BF16).reshape(frames, height, width, 128)

    def place(shard):
        t0 = pay[shard, chunks * rows : (chunks + 1) * rows, :].astype(F32)
        pack = pay[shard, (chunks + 1) * rows :, :].astype(F32)
        plow = low[:half]
        t1 = jnp.concatenate(
            [jnp.where(plow, pack, 0.0), half_roll(jnp.where(plow, 0.0, pack))], axis=0
        )
        tiles = (
            (t0, t1),
            (half_roll(jnp.where(low, t0, 0.0)), half_roll(jnp.where(low, t1, t0))),
        )
        at = pl.ds(shard * frames + 2, frames)
        for b in range(3):
            for v in range(2):
                for n in range(2):
                    ext[v, b, at, 1 : 1 + height, :, n * 128 : (n + 1) * 128] = blocks(
                        shifted(tiles[v][n], width, b)
                    )
        turned = jnp.concatenate(
            [
                jnp.transpose(pay[shard, m * rows : (m + 1) * rows, :])
                for m in range(chunks)
            ],
            axis=0,
        )
        if fused:
            for d in range(chips):
                for e in range(2):
                    at_row = (e * chips + d) * per
                    from_row = (d * 2 + e) * per
                    cot_t[shard, at_row : at_row + per, :] = turned[from_row : from_row + per]
        else:
            cot_t[shard] = turned

    def place_cot(shard, frame):
        for m in range(chunks):
            tile = pay[shard, m * rows : (m + 1) * rows, :].astype(F32)
            for b in range(3):
                cext[b, frame : frame + frames, 1 : 1 + height, :, m * 128 : (m + 1) * 128] = blocks(
                    shifted(tile, width, b)
                )

    place(z)
    place_cot(z, 0)

    def finish_step(step):
        @pl.when(z - 1 - step >= 0)
        def _():
            to_right(step, z - 1 - step).wait_recv()

        @pl.when(z + 1 + step <= tm - 1)
        def _():
            to_left(step, z + 1 + step).wait_recv()

        if step + 1 < tm - 1:
            start_step(step + 1)

        @pl.when(z - 1 - step >= 0)
        def _():
            place(z - 1 - step)

        @pl.when(z + 1 + step <= tm - 1)
        def _():
            place(z + 1 + step)
            if step == 0:
                place_cot(z + 1, frames)

    def pair_tiles(one, two, at, count):
        n = count * pixels

        def part(v, tap):
            k, a, b = tap
            block = ext[v, b, pl.ds(at + k, count), pl.ds(a, height), :, :]
            scale = mask[k, pl.ds(at, count)].reshape(n, 128)
            block = block.reshape(n, 256)
            return block[:, :128] * scale, block[:, 128:] * scale

        a0, a1 = part(0, one)
        if two is None:
            return [a0, a1[:, : cin - 128]]
        b0, b1 = part(1, two)
        return [a0, a1 + b0, b1]

    def conv_some(taps):
        tiles = []
        for n in range(0, len(taps), 2):
            two = taps[n + 1] if n + 1 < len(taps) else None
            tiles += pair_tiles(split(taps[n]), None if two is None else split(two), z * frames, frames)
        return jnp.dot(
            jnp.concatenate(tiles, axis=1),
            w_ref[taps[0] * cin : (taps[-1] + 1) * cin, :],
            preferred_element_type=F32,
        )

    def split(tap):
        return tap // 9, tap // 3 % 3, tap % 3

    finish_step(0)
    w_copy.wait()
    groups = [list(range(n, min(n + 4, 27))) for n in range(0, 27, 4)]
    steps_left = max(tm - 2, 1)
    conv = jnp.zeros((rows, cout), F32)
    done = 0
    for step in range(1, tm):
        upto = len(groups) * step // steps_left if step <= steps_left else len(groups)
        while done < upto:
            conv = conv + conv_some(groups[done])
            done += 1
        if step < tm - 1:
            finish_step(step)
    conv_ref[...] = conv.astype(BF16)

    first_tap = z * slab // cin
    cot_all = jnp.concatenate([cot_t[s] for s in range(tm)], axis=1)

    def core_copy(p):
        return pltpu.make_async_remote_copy(
            src_ref=d16.at[p, 1 - core], dst_ref=r1.at[p], send_sem=core_send.at[p],
            recv_sem=core_recv.at[p], device_id=(z, chip * 2 + 1 - core), device_id_type=MESH,
        )

    def chip_copy(p, r):
        there = (chip + r) % chips
        return pltpu.make_async_remote_copy(
            src_ref=s16.at[p, there], dst_ref=r2.at[p, r - 1], send_sem=chip_send.at[p, r - 1],
            recv_sem=chip_recv.at[p, r - 1], device_id=(z, there * 2 + core), device_id_type=MESH,
        )

    def core_sum(p):
        core_copy(p).wait_recv()
        both = d32[p, core] + r1[p].astype(F32)
        both = both.reshape(chips, per, 2 * cin)
        s32[p] = both
        s16[p] = both.astype(BF16)
        for r in range(1, chips):
            chip_copy(p, r).start()

    for p in range(pairs):
        patches = jnp.concatenate(
            pair_tiles(split(first_tap + 2 * p), split(first_tap + 2 * p + 1), 0, total), axis=1
        )
        part = jnp.dot(cot_all, patches, preferred_element_type=F32)
        if fused:
            part = part.reshape(2, chips * per, 2 * cin)
            d32[p] = part
            d16[p] = part.astype(BF16)
            core_copy(p).start()
            if p > 0:
                core_sum(p - 1)
        else:
            gw_ref[:, p * 2 * cin : (p + 1) * 2 * cin] = part

    act_grad = jnp.zeros((rows, cin), F32)
    for tap in range(27):
        k, a, b = split(tap)
        block = cext[2 - b, 2 - k : 2 - k + frames, 2 - a : 2 - a + height, :, :].reshape(rows, cout)
        if k < 2:
            scale = mask[k, pl.ds(z * frames + 2 - k, frames)].reshape(rows, 128)
            block = jnp.concatenate(
                [block[:, m * 128 : (m + 1) * 128] * scale for m in range(chunks)], axis=1
            )
        act_grad = act_grad + lax.dot_general(
            block, w_ref[tap * cin : (tap + 1) * cin, :], (((1,), (1,)), ((), ())),
            preferred_element_type=F32,
        )
        if fused and tap == 2:
            core_sum(pairs - 1)
    d_normed = act_grad * (sig * (1.0 + normed * (1.0 - sig))) * gain
    along = jnp.sum(d_normed * video, axis=1, keepdims=True) / cin
    vgrad_ref[...] = (inv * d_normed - video * (inv * inv * inv * along)).astype(BF16)

    if fused:
        scale = 1.0 / math.sqrt(dp * total * pixels)
        sums = []
        for p in range(pairs):
            own = s32[p, chip]
            for r in range(1, chips):
                chip_copy(p, r).wait_recv()
                own = own + r2[p, r - 1].astype(F32)
            sums.append(own * scale)
        wide = jnp.concatenate(sums, axis=1)
        skip = z * slab - first_tap * cin
        wide = pltpu.roll(wide, pairs * 2 * cin - skip, axis=1)
        gw_ref[...] = wide[:, :slab]
        for p in range(pairs):
            core_copy(p).wait_send()
            for r in range(1, chips):
                chip_copy(p, r).wait_send()

    for step in range(tm - 1):
        @pl.when((z < tm - 1) & (z - step >= 0))
        def _():
            to_right(step, z - step).wait_send()

        @pl.when((z > 0) & (z + step <= tm - 1))
        def _():
            to_left(step, z + step).wait_send()


def shards(sizes, clip_video, clip_ids, norm_gain, conv_weight, out_cotangent):
    tm, dp = sizes
    unused, frames, height, width, cin = clip_video.shape
    krows, cout = conv_weight.shape
    rows = frames * height * width
    total = tm * frames
    slab = krows // tm
    per = cout // dp
    spans = [-(-(z * slab % cin + slab) // cin) for z in range(tm)]
    pairs = (max(spans) + 1) // 2
    fused = per % 16 == 0
    chips = dp // 2
    chunks = cout // 128
    wide = 2 * pairs * cin
    gw_shape = (per, slab) if fused else (cout, wide)
    cfg = (tm, dp, frames, height, width, cin, cout, slab, pairs, fused)
    side = (pairs, 2, cout // 2, 2 * cin) if fused else (1, 2, 8, 128)
    ends = (pairs, chips, per, 2 * cin) if fused else (1, 1, 16, 128)
    vmem = pl.BlockSpec(memory_space=pltpu.VMEM)
    conv, vgrad, gw = pl.pallas_call(
        functools.partial(kernel, cfg),
        out_shape=(
            jax.ShapeDtypeStruct((rows, cout), BF16),
            jax.ShapeDtypeStruct((rows, cin), BF16),
            jax.ShapeDtypeStruct(gw_shape, F32),
        ),
        in_specs=[vmem, pl.BlockSpec(memory_space=pltpu.SMEM), vmem, pl.BlockSpec(memory_space=pl.ANY), vmem],
        out_specs=(vmem, vmem, vmem),
        scratch_shapes=[
            pltpu.VMEM((krows, cout), BF16),
            pltpu.VMEM((tm, (chunks + 1) * rows + rows // 2, 128), BF16),
            pltpu.VMEM((2, 3, total + 3, height + 2, width, 256), BF16),
            pltpu.VMEM((3, 2 * frames, height + 2, width, cout), BF16),
            pltpu.VMEM((4, total + 2, height * width, 128), BF16),
            pltpu.VMEM((tm, cout, rows), BF16),
            pltpu.VMEM(side, F32),
            pltpu.VMEM(side, BF16),
            pltpu.VMEM(side[:1] + side[2:], BF16),
            pltpu.VMEM(ends, BF16),
            pltpu.VMEM(ends, F32),
            pltpu.VMEM(ends, BF16),
            pltpu.SemaphoreType.DMA,
            pltpu.SemaphoreType.DMA((tm,)),
            pltpu.SemaphoreType.DMA((tm,)),
            pltpu.SemaphoreType.DMA((tm,)),
            pltpu.SemaphoreType.DMA((tm,)),
            pltpu.SemaphoreType.DMA((pairs,)),
            pltpu.SemaphoreType.DMA((pairs,)),
            pltpu.SemaphoreType.DMA((pairs, chips)),
            pltpu.SemaphoreType.DMA((pairs, chips)),
        ],
        compiler_params=pltpu.CompilerParams(
            collective_id=0, has_side_effects=True, vmem_limit_bytes=56 * 1024 * 1024
        ),
    )(
        clip_video.reshape(rows, cin),
        clip_ids,
        norm_gain.reshape(1, cin),
        conv_weight,
        out_cotangent.reshape(rows, cout),
    )
    if fused:
        grad_weight = gw.T
    else:
        scale = 1.0 / math.sqrt(dp * total * height * width)
        mine = lax.psum_scatter(gw * scale, "dp", scatter_dimension=0, tiled=True)
        z = lax.axis_index("tm")
        grad_weight = lax.dynamic_slice_in_dim(mine, z * slab % cin, slab, 1).T
    return (
        conv.reshape(1, frames, height, width, cout),
        vgrad.reshape(1, frames, height, width, cin),
        grad_weight,
    )


def solution(mesh):
    in_specs = (
        P("dp", "tm", None, None, None),
        P("dp", None),
        P(),
        P(),
        P("dp", "tm", None, None, None),
    )
    out_specs = (P("dp", "tm", None, None, None), P("dp", "tm", None, None, None), P("tm", "dp"))
    sizes = (mesh.shape["tm"], mesh.shape["dp"])
    return jax.shard_map(
        functools.partial(shards, sizes), mesh=mesh, in_specs=in_specs, out_specs=out_specs, check_vma=False
    )
```

time: 240 us -> 36.2 us (0.15)
  other arithmetic: 98.1 us -> 0 us
  blocking collectives: 44.2 us -> 0 us
  Pallas kernels: 0 us -> 30.7 us
  local copies, waits for them, and re-layouts: 32.2 us -> 4.69 us
  waiting for transfers between devices: 25.9 us -> 0 us
  matrix products: 21.8 us -> 0 us
  between operations: 14.2 us -> 0.64 us
  starting transfers between devices: 2.62 us -> 0 us
    while x104 -> x0, other arithmetic: 72.4 us -> none
    all_gather x3 -> x0, blocking collectives: 44.2 us -> none  [the longest x1 16.2 us: shards(): lax.all_gather(extended[None], 'tm', axis=0, tiled=True)]
    pallas_call x0 -> x1, Pallas kernels: none -> 30.7 us  [shards(): pl.pallas_call(functools.partial(kernel, cfg), out_shape=(jax.ShapeDtypeS...]
    unnamed x2 -> x0, waiting for transfers between devices: 24.2 us -> none
    dot_general x6 -> x0, matrix products: 21.8 us -> none  [the longest x4 13.7 us: slab_term(): return jnp.dot(slab_part.T, cot_rows, preferred_element_type=jnp.float32)]
    unnamed x27 -> x0, other arithmetic: 18.1 us -> none
    reshape x5 -> x0, local copies, waits for them, and re-layouts: 14.2 us -> none  [extract(): return stacked.reshape(frames * height * width, -1)]
    another operation x5 -> x0, local copies, waits for them, and re-layouts: 12.6 us -> none  [extract(): stacked = jnp.stack(taps, axis=3)]
  transfers between devices with their start and end apart: 3 -> 0, of which waited for: 2 -> 0; matrix products, arithmetic and copies ran while one was open for 8% -> 0% of each run, Pallas kernels for 0% -> 0%
where the time goes in v1:
time: 36.2 us; the launch traced here: 36 us
  Pallas kernels  30.7 us (85%)
  local copies, waits for them, and re-layouts  4.69 us (13%)
  between operations  0.64 us (2%)
    pallas_call x1, Pallas kernels, shards(): pl.pallas_call(functools.partial(kernel, cfg), out_shape=(jax.ShapeDtypeS...  30.7 us
    unnamed x3, local copies, waits for them, and re-layouts  4.69 us

profile of v1, /device:TPU:0, one launch (start us, length us, event | category | flops | bytes accessed | tf_op | source)
XLA Modules:
  0.0 36.0 jit_solution(11150335396086287970)
XLA Ops:
  0.6 30.7 %shard_map.76 = (bf16[128,384]{1,0:T(8,128)(2,1)}, bf16[128,192]{1,0:T(8,128)(2,1)}, f32[48,1296]{1,0:T(8,128)}) custom-call(bf16[128,192]{1,0:T(8,128)(2,1)} %bitcast.9, s32[1,8]{1,0:T(1,128)} %ids_ref.1, f32[1,192]{1,0:T(1,128)} %bitcast.11, bf16[5184,384]{1,0:T(8,128)(2,1)} %w_hbm.1, bf16[128,384]{1,0:T(8,128)(2,1)} %bitcast.8), custom_call_target="tpu_custom_call" | custom-call | tf_op jit(solution)/shard_map/pallas_call | solution.py:343
  31.3 1.5 %copy.11 = bf16[1,2,4,16,384]{4,3,2,1,0:T(8,128)(2,1)} copy(bf16[1,2,4,16,384]{4,3,2,1,0:T(8,128)(2,1)} %bitcast.7) | data formatting | bytes 196608
  32.8 1.5 %copy.12 = bf16[1,2,4,16,192]{4,3,2,1,0:T(8,128)(2,1)} copy(bf16[1,2,4,16,192]{4,3,2,1,0:T(8,128)(2,1)} %bitcast.10) | data formatting | bytes 98304
  34.3 1.7 %copy.13 = f32[1296,48]{0,1:T(8,128)} copy(f32[1296,48]{0,1:T(8,128)} %bitcast.6) | data formatting | bytes 497664

commit v2 on v1

--- a/solution.py
+++ b/solution.py
@@ -373,7 +373,7 @@
             pltpu.SemaphoreType.DMA((pairs, chips)),
         ],
         compiler_params=pltpu.CompilerParams(
-            collective_id=0, has_side_effects=True, vmem_limit_bytes=56 * 1024 * 1024
+            collective_id=0, has_side_effects=True, vmem_limit_bytes=51 * 1024 * 1024
         ),
     )(
         clip_video.reshape(rows, cin),

time: 36.2 us -> 35.4 us (0.978)
  Pallas kernels: 30.7 us -> 29.5 us
    pallas_call x1, Pallas kernels: 30.7 us -> 29.5 us  [shards(): pl.pallas_call(functools.partial(kernel, cfg), out_shape=(jax.ShapeDtypeS...]
    unnamed x3 -> x11, local copies, waits for them, and re-layouts: 4.69 us -> 5.03 us
where the time goes in v2:
time: 35.4 us; the launch traced here: 35.2 us
  Pallas kernels  29.5 us (83%)
  local copies, waits for them, and re-layouts  5.03 us (14%)
  between operations  0.65 us (2%)
    pallas_call x1, Pallas kernels, shards(): pl.pallas_call(functools.partial(kernel, cfg), out_shape=(jax.ShapeDtypeS...  29.5 us
    unnamed x11, local copies, waits for them, and re-layouts  5.03 us

profile of v2, /device:TPU:0, one launch (start us, length us, event | category | flops | bytes accessed | tf_op | source)
XLA Modules:
  0.0 35.2 jit_solution(15069173919251498888)
XLA Ops:
  0.6 0.0 copy-start
  0.6 0.9 %copy-done = bf16[1,2,4,16,384]{4,3,2,1,0:T(8,128)(2,1)S(1)} copy-done((bf16[1,2,4,16,384]{4,3,2,1,0:T(8,128)(2,1)S(1)}, bf16[1,2,4,16,384]{4,3,2,1,0:T(8,128)(2,1)}, u32[]{:S(2)}) %copy-start) | copy-done | bytes 98328
  1.5 0.0 copy-start.1
  1.5 0.8 %copy-done.1 = bf16[1,2,4,16,192]{4,3,2,1,0:T(8,128)(2,1)S(1)} copy-done((bf16[1,2,4,16,192]{4,3,2,1,0:T(8,128)(2,1)S(1)}, bf16[1,2,4,16,192]{4,3,2,1,0:T(8,128)(2,1)}, u32[]{:S(2)}) %copy-start.1) | copy-done | bytes 49176
  2.4 0.0 copy-start.2
  2.4 0.7 %copy-done.2 = f32[192]{0:T(256)S(1)} copy-done((f32[192]{0:T(256)S(1)}, f32[192]{0:T(256)}, u32[]{:S(2)}) %copy-start.2) | copy-done | bytes 792
  3.0 0.0 copy-start.3
  3.0 0.7 %copy-done.3 = s32[1,8]{1,0:T(1,128)S(1)} copy-done((s32[1,8]{1,0:T(1,128)S(1)}, s32[1,8]{1,0:T(1,128)}, u32[]{:S(2)}) %copy-start.3) | copy-done | bytes 56
  3.7 29.5 %shard_map.76 = (bf16[128,384]{1,0:T(8,128)(2,1)S(1)}, bf16[128,192]{1,0:T(8,128)(2,1)S(1)}, f32[48,1296]{1,0:T(8,128)S(1)}) custom-call(bf16[128,192]{1,0:T(8,128)(2,1)S(1)} %bitcast.9, s32[1,8]{1,0:T(1,128)S(1)} %copy-done.3, f32[1,192]{1,0:T(1,128)S(1)} %bitcast.11, bf16[5184,384]{1,0:T(8,128)(2,1)} %w_hbm.1, bf16[128,384]{1,0:T(8,128)(2,1)S(1)} %bitcast.8), custom_call_target="tpu_custom_call" | custom-call | tf_op jit(solution)/shard_map/pallas_call | solution.py:343
  33.2 0.6 %copy.11 = bf16[1,2,4,16,384]{4,3,2,1,0:T(8,128)(2,1)} copy(bf16[1,2,4,16,384]{4,3,2,1,0:T(8,128)(2,1)S(1)} %bitcast.7) | data formatting | bytes 196608
  33.8 0.6 %copy.12 = bf16[1,2,4,16,192]{4,3,2,1,0:T(8,128)(2,1)} copy(bf16[1,2,4,16,192]{4,3,2,1,0:T(8,128)(2,1)S(1)} %bitcast.10) | data formatting | bytes 98304
  34.5 0.7 %copy.13 = f32[1296,48]{0,1:T(8,128)} copy(f32[1296,48]{0,1:T(8,128)S(1)} %bitcast.6) | data formatting | bytes 497664
Async XLA Ops:
  0.6 0.9 %copy-start = (bf16[1,2,4,16,384]{4,3,2,1,0:T(8,128)(2,1)S(1)}, bf16[1,2,4,16,384]{4,3,2,1,0:T(8,128)(2,1)}, u32[]{:S(2)}) copy-start(bf16[1,2,4,16,384]{4,3,2,1,0:T(8,128)(2,1)} %param.9) | copy-start | bytes 294916
  1.5 0.8 %copy-start.1 = (bf16[1,2,4,16,192]{4,3,2,1,0:T(8,128)(2,1)S(1)}, bf16[1,2,4,16,192]{4,3,2,1,0:T(8,128)(2,1)}, u32[]{:S(2)}) copy-start(bf16[1,2,4,16,192]{4,3,2,1,0:T(8,128)(2,1)} %param.5) | copy-start | bytes 147460
  2.4 0.7 %copy-start.2 = (f32[192]{0:T(256)S(1)}, f32[192]{0:T(256)}, u32[]{:S(2)}) copy-start(f32[192]{0:T(256)} %param.7) | copy-start | bytes 2308
  3.0 0.7 %copy-start.3 = (s32[1,8]{1,0:T(1,128)S(1)}, s32[1,8]{1,0:T(1,128)}, u32[]{:S(2)}) copy-start(s32[1,8]{1,0:T(1,128)} %ids_ref.1) | copy-start | bytes 100

commit v3 on v2

--- a/solution.py
+++ b/solution.py
@@ -77,41 +77,53 @@
     first = act[:, :128]
     second = jnp.concatenate([act[:, 128:], jnp.zeros((rows, 64), F32)], axis=1)
     half = rows // 2
-    for m in range(chunks):
-        pay[z, m * rows : (m + 1) * rows, :] = cot_ref[:, m * 128 : (m + 1) * 128]
-    pay[z, chunks * rows : (chunks + 1) * rows, :] = first.astype(BF16)
-    pay[z, (chunks + 1) * rows :, :] = (second[:half] + half_roll(second[half:])).astype(BF16)
+    turned = jnp.concatenate(
+        [jnp.transpose(cot_ref[:, m * 128 : (m + 1) * 128]) for m in range(chunks)], axis=0
+    )
+    order = [(d * 2 + e) * per for e in range(2) for d in range(chips)] if fused else [0]
+    span = per if fused else cout
+    for at_row, from_row in enumerate(order):
+        pay[z, at_row * span : (at_row + 1) * span, :] = turned[from_row : from_row + span]
+    pay[z, cout : cout + rows, :] = first.astype(BF16)
+    pay[z, cout + rows :, :] = (second[:half] + half_roll(second[half:])).astype(BF16)
 
     peers = jnp.where(z > 0, 1, 0) + jnp.where(z < tm - 1, 1, 0)
     if fused:
         peers = peers + chips
     pl.semaphore_wait(barrier, peers)
 
-    def to_right(step, shard):
+    size = pay.shape[1] // 2
+
+    def part_of(shard, h):
+        return pay.at[shard, pl.ds(h * size, size)]
+
+    def to_right(step, shard, h):
         return pltpu.make_async_remote_copy(
-            src_ref=pay.at[shard], dst_ref=pay.at[shard], send_sem=send_r.at[step],
-            recv_sem=recv_r.at[step], device_id=(z + 1, j), device_id_type=MESH,
-        )
-
-    def to_left(step, shard):
+            src_ref=part_of(shard, h), dst_ref=part_of(shard, h), send_sem=send_r.at[step, h],
+            recv_sem=recv_r.at[step, h], device_id=(z + 1, j), device_id_type=MESH,
+        )
+
+    def to_left(step, shard, h):
         return pltpu.make_async_remote_copy(
-            src_ref=pay.at[shard], dst_ref=pay.at[shard], send_sem=send_l.at[step],
-            recv_sem=recv_l.at[step], device_id=(z - 1, j), device_id_type=MESH,
-        )
-
-    def start_step(step):
+            src_ref=part_of(shard, h), dst_ref=part_of(shard, h), send_sem=send_l.at[step, h],
+            recv_sem=recv_l.at[step, h], device_id=(z - 1, j), device_id_type=MESH,
+        )
+
+    def start_step(step, h):
         @pl.when((z < tm - 1) & (z - step >= 0))
         def _():
-            to_right(step, z - step).start()
+            to_right(step, z - step, h).start()
 
         @pl.when((z > 0) & (z + step <= tm - 1))
         def _():
-            to_left(step, z + step).start()
-
-    start_step(0)
+            to_left(step, z + step, h).start()
+
+    start_step(0, 0)
+    start_step(0, 1)
 
     ext[...] = jnp.zeros(ext.shape, BF16)
     cext[...] = jnp.zeros(cext.shape, BF16)
+    cot_t[...] = jnp.zeros(cot_t.shape, BF16)
     mask[...] = jnp.zeros(mask.shape, BF16)
     for t in range(total):
         for k in range(3):
@@ -123,8 +135,8 @@
         return x.astype(BF16).reshape(frames, height, width, 128)
 
     def place(shard):
-        t0 = pay[shard, chunks * rows : (chunks + 1) * rows, :].astype(F32)
-        pack = pay[shard, (chunks + 1) * rows :, :].astype(F32)
+        t0 = pay[shard, cout : cout + rows, :].astype(F32)
+        pack = pay[shard, cout + rows :, :].astype(F32)
         plow = low[:half]
         t1 = jnp.concatenate(
             [jnp.where(plow, pack, 0.0), half_roll(jnp.where(plow, 0.0, pack))], axis=0
@@ -140,44 +152,36 @@
                     ext[v, b, at, 1 : 1 + height, :, n * 128 : (n + 1) * 128] = blocks(
                         shifted(tiles[v][n], width, b)
                     )
-        turned = jnp.concatenate(
-            [
-                jnp.transpose(pay[shard, m * rows : (m + 1) * rows, :])
-                for m in range(chunks)
-            ],
-            axis=0,
-        )
-        if fused:
-            for d in range(chips):
-                for e in range(2):
-                    at_row = (e * chips + d) * per
-                    from_row = (d * 2 + e) * per
-                    cot_t[shard, at_row : at_row + per, :] = turned[from_row : from_row + per]
-        else:
-            cot_t[shard] = turned
-
-    def place_cot(shard, frame):
+        cot_t[shard] = pay[shard, :cout, :]
+
+    def place_cot(tiles, frame):
         for m in range(chunks):
-            tile = pay[shard, m * rows : (m + 1) * rows, :].astype(F32)
+            tile = tiles[m].astype(F32)
             for b in range(3):
                 cext[b, frame : frame + frames, 1 : 1 + height, :, m * 128 : (m + 1) * 128] = blocks(
                     shifted(tile, width, b)
                 )
 
+    def next_tiles():
+        rows_of = {at: pay[z + 1, n * span : (n + 1) * span, :] for n, at in enumerate(order)}
+        natural = jnp.concatenate([rows_of[at] for at in sorted(rows_of)], axis=0)
+        return [jnp.transpose(natural[m * 128 : (m + 1) * 128]) for m in range(chunks)]
+
     place(z)
-    place_cot(z, 0)
+    place_cot([cot_ref[:, m * 128 : (m + 1) * 128] for m in range(chunks)], 0)
 
     def finish_step(step):
-        @pl.when(z - 1 - step >= 0)
-        def _():
-            to_right(step, z - 1 - step).wait_recv()
-
-        @pl.when(z + 1 + step <= tm - 1)
-        def _():
-            to_left(step, z + 1 + step).wait_recv()
-
-        if step + 1 < tm - 1:
-            start_step(step + 1)
+        for h in range(2):
+            @pl.when(z - 1 - step >= 0)
+            def _():
+                to_right(step, z - 1 - step, h).wait_recv()
+
+            @pl.when(z + 1 + step <= tm - 1)
+            def _():
+                to_left(step, z + 1 + step, h).wait_recv()
+
+            if step + 1 < tm - 1:
+                start_step(step + 1, h)
 
         @pl.when(z - 1 - step >= 0)
         def _():
@@ -187,7 +191,7 @@
         def _():
             place(z + 1 + step)
             if step == 0:
-                place_cot(z + 1, frames)
+                place_cot(next_tiles(), frames)
 
     def pair_tiles(one, two, at, count):
         n = count * pixels
@@ -219,27 +223,42 @@
     def split(tap):
         return tap // 9, tap // 3 % 3, tap % 3
 
+    def conv_range(start, stop):
+        found = jnp.zeros((rows, cout), F32)
+        for n in range(start, stop, 4):
+            found = found + conv_some(list(range(n, min(n + 4, stop))))
+        return found
+
+    def grad_range(start, stop):
+        found = jnp.zeros((rows, cin), F32)
+        for tap in range(start, stop):
+            k, a, b = split(tap)
+            block = cext[2 - b, 2 - k : 2 - k + frames, 2 - a : 2 - a + height, :, :].reshape(rows, cout)
+            if k < 2:
+                scale = mask[k, pl.ds(z * frames + 2 - k, frames)].reshape(rows, 128)
+                block = jnp.concatenate(
+                    [block[:, m * 128 : (m + 1) * 128] * scale for m in range(chunks)], axis=1
+                )
+            found = found + lax.dot_general(
+                block, w_ref[tap * cin : (tap + 1) * cin, :], (((1,), (1,)), ((), ())),
+                preferred_element_type=F32,
+            )
+        return found
+
+    w_copy.wait()
+    conv = conv_range(18, 27)
+    act_grad = grad_range(18, 27)
     finish_step(0)
-    w_copy.wait()
-    groups = [list(range(n, min(n + 4, 27))) for n in range(0, 27, 4)]
-    steps_left = max(tm - 2, 1)
-    conv = jnp.zeros((rows, cout), F32)
-    done = 0
-    for step in range(1, tm):
-        upto = len(groups) * step // steps_left if step <= steps_left else len(groups)
-        while done < upto:
-            conv = conv + conv_some(groups[done])
-            done += 1
-        if step < tm - 1:
-            finish_step(step)
+    conv = conv + conv_range(0, 18)
     conv_ref[...] = conv.astype(BF16)
+    for step in range(1, tm - 2):
+        finish_step(step)
 
     first_tap = z * slab // cin
-    cot_all = jnp.concatenate([cot_t[s] for s in range(tm)], axis=1)
 
     def core_copy(p):
         return pltpu.make_async_remote_copy(
-            src_ref=d16.at[p, 1 - core], dst_ref=r1.at[p], send_sem=core_send.at[p],
+            src_ref=d16.at[p], dst_ref=r1.at[p], send_sem=core_send.at[p],
             recv_sem=core_recv.at[p], device_id=(z, chip * 2 + 1 - core), device_id_type=MESH,
         )
 
@@ -259,36 +278,32 @@
         for r in range(1, chips):
             chip_copy(p, r).start()
 
+    def weight_part(p, cot_rows, at, count):
+        one = first_tap + 2 * p
+        patches = jnp.concatenate(pair_tiles(split(one), split(one + 1), at, count), axis=1)
+        return jnp.dot(cot_rows, patches, preferred_element_type=F32).reshape(d32.shape[1:])
+
+    cot_all = jnp.concatenate([cot_t[s] for s in range(tm)], axis=1)
     for p in range(pairs):
-        patches = jnp.concatenate(
-            pair_tiles(split(first_tap + 2 * p), split(first_tap + 2 * p + 1), 0, total), axis=1
-        )
-        part = jnp.dot(cot_all, patches, preferred_element_type=F32)
+        d32[p] = weight_part(p, cot_all, 0, total)
+    finish_step(tm - 2)
+    last = tm - 1 - z
+    for p in range(pairs):
+        @pl.when((z == 0) | (z == tm - 1))
+        def _():
+            d32[p] = d32[p] + weight_part(p, cot_t[last], last * frames, frames)
+
         if fused:
-            part = part.reshape(2, chips * per, 2 * cin)
-            d32[p] = part
-            d16[p] = part.astype(BF16)
+            d16[p] = d32[p, 1 - core].astype(BF16)
             core_copy(p).start()
             if p > 0:
                 core_sum(p - 1)
         else:
-            gw_ref[:, p * 2 * cin : (p + 1) * 2 * cin] = part
-
-    act_grad = jnp.zeros((rows, cin), F32)
-    for tap in range(27):
-        k, a, b = split(tap)
-        block = cext[2 - b, 2 - k : 2 - k + frames, 2 - a : 2 - a + height, :, :].reshape(rows, cout)
-        if k < 2:
-            scale = mask[k, pl.ds(z * frames + 2 - k, frames)].reshape(rows, 128)
-            block = jnp.concatenate(
-                [block[:, m * 128 : (m + 1) * 128] * scale for m in range(chunks)], axis=1
-            )
-        act_grad = act_grad + lax.dot_general(
-            block, w_ref[tap * cin : (tap + 1) * cin, :], (((1,), (1,)), ((), ())),
-            preferred_element_type=F32,
-        )
-        if fused and tap == 2:
-            core_sum(pairs - 1)
+            gw_ref[:, p * 2 * cin : (p + 1) * 2 * cin] = d32[p].reshape(cout, 2 * cin)
+    act_grad = act_grad + grad_range(0, 3)
+    if fused:
+        core_sum(pairs - 1)
+    act_grad = act_grad + grad_range(3, 18)
     d_normed = act_grad * (sig * (1.0 + normed * (1.0 - sig))) * gain
     along = jnp.sum(d_normed * video, axis=1, keepdims=True) / cin
     vgrad_ref[...] = (inv * d_normed - video * (inv * inv * inv * along)).astype(BF16)
@@ -314,11 +329,13 @@
     for step in range(tm - 1):
         @pl.when((z < tm - 1) & (z - step >= 0))
         def _():
-            to_right(step, z - step).wait_send()
+            for h in range(2):
+                to_right(step, z - step, h).wait_send()
 
         @pl.when((z > 0) & (z + step <= tm - 1))
         def _():
-            to_left(step, z + step).wait_send()
+            for h in range(2):
+                to_left(step, z + step, h).wait_send()
 
 
 def shards(sizes, clip_video, clip_ids, norm_gain, conv_weight, out_cotangent):
@@ -337,9 +354,21 @@
     wide = 2 * pairs * cin
     gw_shape = (per, slab) if fused else (cout, wide)
     cfg = (tm, dp, frames, height, width, cin, cout, slab, pairs, fused)
-    side = (pairs, 2, cout // 2, 2 * cin) if fused else (1, 2, 8, 128)
+    side = (pairs, 2, cout // 2, 2 * cin)
+    one_side = (pairs, cout // 2, 2 * cin) if fused else (1, 16, 128)
     ends = (pairs, chips, per, 2 * cin) if fused else (1, 1, 16, 128)
     vmem = pl.BlockSpec(memory_space=pltpu.VMEM)
+    hbm = pltpu.HBM
+    pinned = [
+        pltpu.with_memory_space_constraint(x, hbm)
+        for x in (
+            clip_video.reshape(rows, cin),
+            norm_gain.reshape(1, cin),
+            conv_weight,
+            out_cotangent.reshape(rows, cout),
+            clip_ids,
+        )
+    ]
     conv, vgrad, gw = pl.pallas_call(
         functools.partial(kernel, cfg),
         out_shape=(
@@ -357,30 +386,28 @@
             pltpu.VMEM((4, total + 2, height * width, 128), BF16),
             pltpu.VMEM((tm, cout, rows), BF16),
             pltpu.VMEM(side, F32),
-            pltpu.VMEM(side, BF16),
-            pltpu.VMEM(side[:1] + side[2:], BF16),
+            pltpu.VMEM(one_side, BF16),
+            pltpu.VMEM(one_side, BF16),
             pltpu.VMEM(ends, BF16),
             pltpu.VMEM(ends, F32),
             pltpu.VMEM(ends, BF16),
             pltpu.SemaphoreType.DMA,
-            pltpu.SemaphoreType.DMA((tm,)),
-            pltpu.SemaphoreType.DMA((tm,)),
-            pltpu.SemaphoreType.DMA((tm,)),
-            pltpu.SemaphoreType.DMA((tm,)),
+            pltpu.SemaphoreType.DMA((tm, 2)),
+            pltpu.SemaphoreType.DMA((tm, 2)),
+            pltpu.SemaphoreType.DMA((tm, 2)),
+            pltpu.SemaphoreType.DMA((tm, 2)),
             pltpu.SemaphoreType.DMA((pairs,)),
             pltpu.SemaphoreType.DMA((pairs,)),
             pltpu.SemaphoreType.DMA((pairs, chips)),
             pltpu.SemaphoreType.DMA((pairs, chips)),
         ],
         compiler_params=pltpu.CompilerParams(
-            collective_id=0, has_side_effects=True, vmem_limit_bytes=51 * 1024 * 1024
+            collective_id=0, has_side_effects=True, vmem_limit_bytes=40 * 1024 * 1024
         ),
     )(
-        clip_video.reshape(rows, cin),
-        clip_ids,
-        norm_gain.reshape(1, cin),
-        conv_weight,
-        out_cotangent.reshape(rows, cout),
+        pinned[0],
+        pinned[4],
+        *pinned[1:4],
     )
     if fused:
         grad_weight = gw.T

time: 35.4 us -> 30.3 us (0.86)
  local copies, waits for them, and re-layouts: 5.03 us -> 1.98 us
  Pallas kernels: 29.5 us -> 27.5 us
    unnamed x11 -> x3, local copies, waits for them, and re-layouts: 5.03 us -> 1.98 us
    pallas_call x1, Pallas kernels: 29.5 us -> 27.5 us  [shards(): pl.pallas_call(functools.partial(kernel, cfg), out_shape=(jax.ShapeDtypeS...]
where the time goes in v3:
time: 30.3 us; the launch traced here: 30.1 us
  Pallas kernels  27.5 us (91%)
  local copies, waits for them, and re-layouts  1.98 us (7%)
  between operations  0.64 us (2%)
    pallas_call x1, Pallas kernels, shards(): pl.pallas_call(functools.partial(kernel, cfg), out_shape=(jax.ShapeDtypeS...  27.5 us
    unnamed x3, local copies, waits for them, and re-layouts  1.98 us

profile of v3, /device:TPU:0, one launch (start us, length us, event | category | flops | bytes accessed | tf_op | source)
XLA Modules:
  0.0 30.1 jit_solution(7563421414513958999)
XLA Ops:
  0.6 27.5 %shard_map.76 = (bf16[128,384]{1,0:T(8,128)(2,1)S(1)}, bf16[128,192]{1,0:T(8,128)(2,1)S(1)}, f32[48,1296]{1,0:T(8,128)S(1)}) custom-call(bf16[128,192]{1,0:T(8,128)(2,1)} %bitcast.10, s32[1,8]{1,0:T(1,128)} %ids_ref.1, f32[1,192]{1,0:T(1,128)} %bitcast.11, bf16[5184,384]{1,0:T(8,128)(2,1)} %w_hbm.1, bf16[128,384]{1,0:T(8,128)(2,1)} %bitcast.9), custom_call_target="tpu_custom_call" | custom-call | tf_op jit(solution)/shard_map/pallas_call | solution.py:372
  28.1 0.6 %copy.11 = bf16[1,2,4,16,384]{4,3,2,1,0:T(8,128)(2,1)} copy(bf16[1,2,4,16,384]{4,3,2,1,0:T(8,128)(2,1)S(1)} %bitcast.7) | data formatting | bytes 196608
  28.8 0.6 %copy.12 = bf16[1,2,4,16,192]{4,3,2,1,0:T(8,128)(2,1)} copy(bf16[1,2,4,16,192]{4,3,2,1,0:T(8,128)(2,1)S(1)} %bitcast.8) | data formatting | bytes 98304
  29.4 0.7 %copy.13 = f32[1296,48]{0,1:T(8,128)} copy(f32[1296,48]{0,1:T(8,128)S(1)} %bitcast.6) | data formatting | bytes 497664

commit v4 on v3

--- a/solution.py
+++ b/solution.py
@@ -170,19 +170,19 @@
     place(z)
     place_cot([cot_ref[:, m * 128 : (m + 1) * 128] for m in range(chunks)], 0)
 
-    def finish_step(step):
-        for h in range(2):
-            @pl.when(z - 1 - step >= 0)
-            def _():
-                to_right(step, z - 1 - step, h).wait_recv()
-
-            @pl.when(z + 1 + step <= tm - 1)
-            def _():
-                to_left(step, z + 1 + step, h).wait_recv()
-
-            if step + 1 < tm - 1:
-                start_step(step + 1, h)
-
+    def pass_on(step, h):
+        @pl.when(z - 1 - step >= 0)
+        def _():
+            to_right(step, z - 1 - step, h).wait_recv()
+
+        @pl.when(z + 1 + step <= tm - 1)
+        def _():
+            to_left(step, z + 1 + step, h).wait_recv()
+
+        if step + 1 < tm - 1:
+            start_step(step + 1, h)
+
+    def lay_out(step):
         @pl.when(z - 1 - step >= 0)
         def _():
             place(z - 1 - step)
@@ -231,28 +231,41 @@
 
     def grad_range(start, stop):
         found = jnp.zeros((rows, cin), F32)
-        for tap in range(start, stop):
+
+        def columns(tap):
             k, a, b = split(tap)
             block = cext[2 - b, 2 - k : 2 - k + frames, 2 - a : 2 - a + height, :, :].reshape(rows, cout)
-            if k < 2:
-                scale = mask[k, pl.ds(z * frames + 2 - k, frames)].reshape(rows, 128)
-                block = jnp.concatenate(
-                    [block[:, m * 128 : (m + 1) * 128] * scale for m in range(chunks)], axis=1
-                )
+            if k == 2:
+                return [block]
+            scale = mask[k, pl.ds(z * frames + 2 - k, frames)].reshape(rows, 128)
+            return [block[:, m * 128 : (m + 1) * 128] * scale for m in range(chunks)]
+
+        for first in range(start, stop, 2):
+            taps = range(first, min(first + 2, stop))
             found = found + lax.dot_general(
-                block, w_ref[tap * cin : (tap + 1) * cin, :], (((1,), (1,)), ((), ())),
+                jnp.concatenate([tile for tap in taps for tile in columns(tap)], axis=1),
+                jnp.concatenate([w_ref[tap * cin : (tap + 1) * cin, :] for tap in taps], axis=1),
+                (((1,), (1,)), ((), ())),
                 preferred_element_type=F32,
             )
         return found
 
     w_copy.wait()
     conv = conv_range(18, 27)
-    act_grad = grad_range(18, 27)
-    finish_step(0)
-    conv = conv + conv_range(0, 18)
-    conv_ref[...] = conv.astype(BF16)
+    pass_on(0, 0)
+    act_grad = grad_range(18, 24)
+    pass_on(0, 1)
+    lay_out(0)
+    conv = conv + conv_range(0, 8)
+    if tm > 3:
+        pass_on(1, 0)
+    conv = conv + conv_range(8, 16)
     for step in range(1, tm - 2):
-        finish_step(step)
+        if step > 1:
+            pass_on(step, 0)
+        pass_on(step, 1)
+        lay_out(step)
+    conv_ref[...] = (conv + conv_range(16, 18)).astype(BF16)
 
     first_tap = z * slab // cin
 
@@ -283,15 +296,22 @@
         patches = jnp.concatenate(pair_tiles(split(one), split(one + 1), at, count), axis=1)
         return jnp.dot(cot_rows, patches, preferred_element_type=F32).reshape(d32.shape[1:])
 
+    early = max(pairs - 1, 1)
     cot_all = jnp.concatenate([cot_t[s] for s in range(tm)], axis=1)
-    for p in range(pairs):
+    for p in range(early):
         d32[p] = weight_part(p, cot_all, 0, total)
-    finish_step(tm - 2)
+    pass_on(tm - 2, 0)
+    pass_on(tm - 2, 1)
+    lay_out(tm - 2)
     last = tm - 1 - z
     for p in range(pairs):
-        @pl.when((z == 0) | (z == tm - 1))
-        def _():
-            d32[p] = d32[p] + weight_part(p, cot_t[last], last * frames, frames)
+        if p < early:
+            @pl.when((z == 0) | (z == tm - 1))
+            def _():
+                d32[p] = d32[p] + weight_part(p, cot_t[last], last * frames, frames)
+        else:
+            cot_all = jnp.concatenate([cot_t[s] for s in range(tm)], axis=1)
+            d32[p] = weight_part(p, cot_all, 0, total)
 
         if fused:
             d16[p] = d32[p, 1 - core].astype(BF16)
@@ -300,10 +320,10 @@
                 core_sum(p - 1)
         else:
             gw_ref[:, p * 2 * cin : (p + 1) * 2 * cin] = d32[p].reshape(cout, 2 * cin)
-    act_grad = act_grad + grad_range(0, 3)
+    act_grad = act_grad + grad_range(24, 27)
     if fused:
         core_sum(pairs - 1)
-    act_grad = act_grad + grad_range(3, 18)
+    act_grad = act_grad + grad_range(0, 18)
     d_normed = act_grad * (sig * (1.0 + normed * (1.0 - sig))) * gain
     along = jnp.sum(d_normed * video, axis=1, keepdims=True) / cin
     vgrad_ref[...] = (inv * d_normed - video * (inv * inv * inv * along)).astype(BF16)
@@ -336,6 +356,16 @@
         def _():
             for h in range(2):
                 to_left(step, z + step, h).wait_send()
+
+
+def emit(*refs):
+    count = len(refs) // 2
+    sems = refs[-1]
+    copies = [pltpu.make_async_copy(refs[n], refs[count + n], sems.at[n]) for n in range(count)]
+    for copy in copies:
+        copy.start()
+    for copy in copies:
+        copy.wait()
 
 
 def shards(sizes, clip_video, clip_ids, norm_gain, conv_weight, out_cotangent):
@@ -409,6 +439,15 @@
         pinned[4],
         *pinned[1:4],
     )
+    results = (conv, vgrad, gw)
+    conv, vgrad, gw = pl.pallas_call(
+        emit,
+        out_shape=tuple(jax.ShapeDtypeStruct(x.shape, x.dtype) for x in results),
+        in_specs=[pl.BlockSpec(memory_space=pl.ANY)] * 3,
+        out_specs=(pl.BlockSpec(memory_space=pl.ANY),) * 3,
+        scratch_shapes=[pltpu.SemaphoreType.DMA((3,))],
+        compiler_params=pltpu.CompilerParams(vmem_limit_bytes=1024 * 1024),
+    )(*results)
     if fused:
         grad_weight = gw.T
     else:

time: 30.3 us -> 29.1 us (0.960)
  local copies, waits for them, and re-layouts: 1.98 us -> 0 us
  Pallas kernels: 27.5 us -> 28.3 us
    unnamed x3 -> x0, local copies, waits for them, and re-layouts: 1.98 us -> none
    pallas_call x0 -> x1, Pallas kernels: none -> 0.79 us  [shards(): pl.pallas_call(emit, out_shape=tuple((jax.ShapeDtypeStruct(x.shape, x.dty...]
where the time goes in v4:
time: 29.1 us; the launch traced here: 28.9 us
  Pallas kernels  28.3 us (97%)
  between operations  0.64 us (2%)
    pallas_call x1, Pallas kernels, shards(): pl.pallas_call(functools.partial(kernel, cfg), out_shape=(jax.ShapeDtypeS...  27.5 us
    pallas_call x1, Pallas kernels, shards(): pl.pallas_call(emit, out_shape=tuple((jax.ShapeDtypeStruct(x.shape, x.dty...  0.79 us

profile of v4, /device:TPU:0, one launch (start us, length us, event | category | flops | bytes accessed | tf_op | source)
XLA Modules:
  0.0 28.9 jit_solution(6442276117953160468)
XLA Ops:
  0.6 27.5 %shard_map.76 = (bf16[128,384]{1,0:T(8,128)(2,1)S(1)}, bf16[128,192]{1,0:T(8,128)(2,1)S(1)}, f32[48,1296]{1,0:T(8,128)S(1)}) custom-call(bf16[128,192]{1,0:T(8,128)(2,1)} %bitcast.7, s32[1,8]{1,0:T(1,128)} %ids_ref.1, f32[1,192]{1,0:T(1,128)} %bitcast.8, bf16[5184,384]{1,0:T(8,128)(2,1)} %w_hbm.1, bf16[128,384]{1,0:T(8,128)(2,1)} %bitcast.6), custom_call_target="tpu_custom_call" | custom-call | tf_op jit(solution)/shard_map/pallas_call | solution.py:402
  28.1 0.8 %shard_map.77 = (bf16[128,384]{1,0:T(8,128)(2,1)}, bf16[128,192]{1,0:T(8,128)(2,1)}, f32[48,1296]{1,0:T(8,128)}) custom-call(bf16[128,384]{1,0:T(8,128)(2,1)S(1)} %get-tuple-element.9.refs_0_, bf16[128,192]{1,0:T(8,128)(2,1)S(1)} %get-tuple-element.10.refs_1_, f32[48,1296]{1,0:T(8,128)S(1)} %get-tuple-element.11.refs_2_), custom_call_target="tpu_custom_call" | custom-call | tf_op jit(solution)/shard_map/pallas_call | solution.py:443

commit v5 on v4

--- a/solution.py
+++ b/solution.py
@@ -29,7 +29,7 @@
 
 def kernel(
     cfg, video_ref, ids_ref, gain_ref, w_hbm, cot_ref, conv_ref, vgrad_ref, gw_ref,
-    w_ref, pay, ext, cext, mask, cot_t, d32, d16, r1, s16, s32, r2,
+    w_ref, conv_sum, grad_sum, pay, ext, cext, mask, cot_t, d32, d16, r1, s16, s32, r2,
     w_sem, send_r, send_l, recv_r, recv_l, core_send, core_recv, chip_send, chip_recv,
 ):
     tm, dp, frames, height, width, cin, cout, slab, pairs, fused = cfg
@@ -44,7 +44,7 @@
     chips = dp // 2
     per = cout // dp
 
-    w_copy = pltpu.make_async_copy(w_hbm, w_ref, w_sem)
+    w_copy = pltpu.make_async_copy(w_hbm, w_ref.at[pl.ds(0, 27 * cin)], w_sem)
     w_copy.start()
 
     barrier = pltpu.get_barrier_semaphore()
@@ -121,10 +121,26 @@
     start_step(0, 0)
     start_step(0, 1)
 
-    ext[...] = jnp.zeros(ext.shape, BF16)
-    cext[...] = jnp.zeros(cext.shape, BF16)
-    cot_t[...] = jnp.zeros(cot_t.shape, BF16)
-    mask[...] = jnp.zeros(mask.shape, BF16)
+    def each(start, stop, body):
+        def step(n, unused):
+            body(n)
+            return unused
+
+        lax.fori_loop(start, stop, step, 0)
+
+    def clear(ref):
+        def body(n):
+            ref[n] = jnp.zeros(ref.shape[1:], BF16)
+
+        each(0, ref.shape[0], body)
+
+    clear(ext)
+    clear(cext)
+    clear(cot_t)
+    clear(mask)
+    w_ref[27 * cin :, :] = jnp.zeros((cin, cout), BF16)
+    conv_sum[...] = jnp.zeros(conv_sum.shape, F32)
+    grad_sum[...] = jnp.zeros(grad_sum.shape, F32)
     for t in range(total):
         for k in range(3):
             if t - 2 + k >= 0:
@@ -149,7 +165,7 @@
         for b in range(3):
             for v in range(2):
                 for n in range(2):
-                    ext[v, b, at, 1 : 1 + height, :, n * 128 : (n + 1) * 128] = blocks(
+                    ext[v * 3 + b, at, 1 : 1 + height, :, n * 128 : (n + 1) * 128] = blocks(
                         shifted(tiles[v][n], width, b)
                     )
         cot_t[shard] = pay[shard, :cout, :]
@@ -183,14 +199,17 @@
             start_step(step + 1, h)
 
     def lay_out(step):
-        @pl.when(z - 1 - step >= 0)
-        def _():
-            place(z - 1 - step)
-
-        @pl.when(z + 1 + step <= tm - 1)
-        def _():
-            place(z + 1 + step)
-            if step == 0:
+        def side(n):
+            shard = z + (2 * n - 1) * (1 + step)
+
+            @pl.when((shard >= 0) & (shard <= tm - 1))
+            def _():
+                place(shard)
+
+        each(0, 2, side)
+        if step == 0:
+            @pl.when(z + 1 <= tm - 1)
+            def _():
                 place_cot(next_tiles(), frames)
 
     def pair_tiles(one, two, at, count):
@@ -198,7 +217,7 @@
 
         def part(v, tap):
             k, a, b = tap
-            block = ext[v, b, pl.ds(at + k, count), pl.ds(a, height), :, :]
+            block = ext[v * 3 + b, pl.ds(at + k, count), pl.ds(a, height), :, :]
             scale = mask[k, pl.ds(at, count)].reshape(n, 128)
             block = block.reshape(n, 256)
             return block[:, :128] * scale, block[:, 128:] * scale
@@ -209,63 +228,44 @@
         b0, b1 = part(1, two)
         return [a0, a1 + b0, b1]
 
-    def conv_some(taps):
-        tiles = []
-        for n in range(0, len(taps), 2):
-            two = taps[n + 1] if n + 1 < len(taps) else None
-            tiles += pair_tiles(split(taps[n]), None if two is None else split(two), z * frames, frames)
-        return jnp.dot(
-            jnp.concatenate(tiles, axis=1),
-            w_ref[taps[0] * cin : (taps[-1] + 1) * cin, :],
-            preferred_element_type=F32,
-        )
-
     def split(tap):
         return tap // 9, tap // 3 % 3, tap % 3
 
-    def conv_range(start, stop):
-        found = jnp.zeros((rows, cout), F32)
-        for n in range(start, stop, 4):
-            found = found + conv_some(list(range(n, min(n + 4, stop))))
-        return found
-
-    def grad_range(start, stop):
-        found = jnp.zeros((rows, cin), F32)
-
-        def columns(tap):
-            k, a, b = split(tap)
-            block = cext[2 - b, 2 - k : 2 - k + frames, 2 - a : 2 - a + height, :, :].reshape(rows, cout)
-            if k == 2:
-                return [block]
-            scale = mask[k, pl.ds(z * frames + 2 - k, frames)].reshape(rows, 128)
-            return [block[:, m * 128 : (m + 1) * 128] * scale for m in range(chunks)]
-
-        for first in range(start, stop, 2):
-            taps = range(first, min(first + 2, stop))
-            found = found + lax.dot_general(
-                jnp.concatenate([tile for tap in taps for tile in columns(tap)], axis=1),
-                jnp.concatenate([w_ref[tap * cin : (tap + 1) * cin, :] for tap in taps], axis=1),
-                (((1,), (1,)), ((), ())),
-                preferred_element_type=F32,
-            )
-        return found
+    def conv_four(n):
+        tap = 4 * n
+        tiles = pair_tiles(split(tap), split(tap + 1), z * frames, frames)
+        tiles += pair_tiles(split(tap + 2), split(tap + 3), z * frames, frames)
+        at = pl.multiple_of(tap * cin, 4 * cin)
+        conv_sum[...] += jnp.dot(
+            jnp.concatenate(tiles, axis=1), w_ref[pl.ds(at, 4 * cin), :], preferred_element_type=F32
+        )
+
+    def grad_three(n):
+        k, a = n // 3, n % 3
+        scale = mask[k, pl.ds(z * frames + 2 - k, frames)].reshape(rows, 128)
+        tiles, weights = [], []
+        for b in range(3):
+            block = cext[2 - b, pl.ds(2 - k, frames), pl.ds(2 - a, height), :, :].reshape(rows, cout)
+            tiles += [block[:, m * 128 : (m + 1) * 128] * scale for m in range(chunks)]
+            at = pl.multiple_of((3 * n + b) * cin, cin)
+            weights.append(w_ref[pl.ds(at, cin), :])
+        grad_sum[...] += lax.dot_general(
+            jnp.concatenate(tiles, axis=1), jnp.concatenate(weights, axis=1),
+            (((1,), (1,)), ((), ())), preferred_element_type=F32,
+        )
 
     w_copy.wait()
-    conv = conv_range(18, 27)
+    each(5, 7, conv_four)
     pass_on(0, 0)
-    act_grad = grad_range(18, 24)
+    each(6, 9, grad_three)
     pass_on(0, 1)
     lay_out(0)
-    conv = conv + conv_range(0, 8)
-    if tm > 3:
-        pass_on(1, 0)
-    conv = conv + conv_range(8, 16)
+    each(0, 5, conv_four)
+    conv_ref[...] = conv_sum[...].astype(BF16)
     for step in range(1, tm - 2):
-        if step > 1:
-            pass_on(step, 0)
+        pass_on(step, 0)
         pass_on(step, 1)
         lay_out(step)
-    conv_ref[...] = (conv + conv_range(16, 18)).astype(BF16)
 
     first_tap = z * slab // cin
 
@@ -296,34 +296,38 @@
         patches = jnp.concatenate(pair_tiles(split(one), split(one + 1), at, count), axis=1)
         return jnp.dot(cot_rows, patches, preferred_element_type=F32).reshape(d32.shape[1:])
 
-    early = max(pairs - 1, 1)
     cot_all = jnp.concatenate([cot_t[s] for s in range(tm)], axis=1)
-    for p in range(early):
+
+    def early(p):
         d32[p] = weight_part(p, cot_all, 0, total)
+
+    each(0, pairs, early)
     pass_on(tm - 2, 0)
     pass_on(tm - 2, 1)
     lay_out(tm - 2)
     last = tm - 1 - z
-    for p in range(pairs):
-        if p < early:
-            @pl.when((z == 0) | (z == tm - 1))
-            def _():
-                d32[p] = d32[p] + weight_part(p, cot_t[last], last * frames, frames)
-        else:
-            cot_all = jnp.concatenate([cot_t[s] for s in range(tm)], axis=1)
-            d32[p] = weight_part(p, cot_all, 0, total)
+
+    def late(p):
+        @pl.when((z == 0) | (z == tm - 1))
+        def _():
+            d32[p] = d32[p] + weight_part(p, cot_t[last], last * frames, frames)
 
         if fused:
             d16[p] = d32[p, 1 - core].astype(BF16)
             core_copy(p).start()
-            if p > 0:
+
+            @pl.when(p > 0)
+            def _():
                 core_sum(p - 1)
-        else:
-            gw_ref[:, p * 2 * cin : (p + 1) * 2 * cin] = d32[p].reshape(cout, 2 * cin)
-    act_grad = act_grad + grad_range(24, 27)
+
+    each(0, pairs, late)
     if fused:
         core_sum(pairs - 1)
-    act_grad = act_grad + grad_range(0, 18)
+    else:
+        for p in range(pairs):
+            gw_ref[:, p * 2 * cin : (p + 1) * 2 * cin] = d32[p].reshape(cout, 2 * cin)
+    each(0, 6, grad_three)
+    act_grad = grad_sum[...]
     d_normed = act_grad * (sig * (1.0 + normed * (1.0 - sig))) * gain
     along = jnp.sum(d_normed * video, axis=1, keepdims=True) / cin
     vgrad_ref[...] = (inv * d_normed - video * (inv * inv * inv * along)).astype(BF16)
@@ -409,9 +413,11 @@
         in_specs=[vmem, pl.BlockSpec(memory_space=pltpu.SMEM), vmem, pl.BlockSpec(memory_space=pl.ANY), vmem],
         out_specs=(vmem, vmem, vmem),
         scratch_shapes=[
-            pltpu.VMEM((krows, cout), BF16),
+            pltpu.VMEM((krows + cin, cout), BF16),
+            pltpu.VMEM((rows, cout), F32),
+            pltpu.VMEM((rows, cin), F32),
             pltpu.VMEM((tm, (chunks + 1) * rows + rows // 2, 128), BF16),
-            pltpu.VMEM((2, 3, total + 3, height + 2, width, 256), BF16),
+            pltpu.VMEM((6, total + 3, height + 2, width, 256), BF16),
             pltpu.VMEM((3, 2 * frames, height + 2, width, cout), BF16),
             pltpu.VMEM((4, total + 2, height * width, 128), BF16),
             pltpu.VMEM((tm, cout, rows), BF16),

time: 29.1 us -> 29.4 us (1.010)
  Pallas kernels: 28.3 us -> 28.6 us
    pallas_call x1, Pallas kernels: 27.5 us -> 27.8 us  [shards(): pl.pallas_call(functools.partial(kernel, cfg), out_shape=(jax.ShapeDtypeS...]
where the time goes in v5:
time: 29.4 us; the launch traced here: 29.2 us
  Pallas kernels  28.6 us (97%)
  between operations  0.64 us (2%)
    pallas_call x1, Pallas kernels, shards(): pl.pallas_call(functools.partial(kernel, cfg), out_shape=(jax.ShapeDtypeS...  27.8 us
    pallas_call x1, Pallas kernels, shards(): pl.pallas_call(emit, out_shape=tuple((jax.ShapeDtypeStruct(x.shape, x.dty...  0.79 us

profile of v5, /device:TPU:0, one launch (start us, length us, event | category | flops | bytes accessed | tf_op | source)
XLA Modules:
  0.0 29.2 jit_solution(16626959487182991195)
XLA Ops:
  0.6 27.8 %shard_map.76 = (bf16[128,384]{1,0:T(8,128)(2,1)S(1)}, bf16[128,192]{1,0:T(8,128)(2,1)S(1)}, f32[48,1296]{1,0:T(8,128)S(1)}) custom-call(bf16[128,192]{1,0:T(8,128)(2,1)} %bitcast.7, s32[1,8]{1,0:T(1,128)} %ids_ref.1, f32[1,192]{1,0:T(1,128)} %bitcast.8, bf16[5184,384]{1,0:T(8,128)(2,1)} %w_hbm.1, bf16[128,384]{1,0:T(8,128)(2,1)} %bitcast.6), custom_call_target="tpu_custom_call" | custom-call | tf_op jit(solution)/shard_map/pallas_call | solution.py:406
  28.4 0.8 %shard_map.77 = (bf16[128,384]{1,0:T(8,128)(2,1)}, bf16[128,192]{1,0:T(8,128)(2,1)}, f32[48,1296]{1,0:T(8,128)}) custom-call(bf16[128,384]{1,0:T(8,128)(2,1)S(1)} %get-tuple-element.9.refs_0_, bf16[128,192]{1,0:T(8,128)(2,1)S(1)} %get-tuple-element.10.refs_1_, f32[48,1296]{1,0:T(8,128)S(1)} %get-tuple-element.11.refs_2_), custom_call_target="tpu_custom_call" | custom-call | tf_op jit(solution)/shard_map/pallas_call | solution.py:449

commit v6 on v5

--- a/solution.py
+++ b/solution.py
@@ -52,13 +52,18 @@
     def greet(where):
         pl.semaphore_signal(barrier, inc=1, device_id=where, device_id_type=MESH)
 
-    @pl.when(z > 0)
-    def _():
-        greet((z - 1, j))
-
-    @pl.when(z < tm - 1)
-    def _():
-        greet((z + 1, j))
+    short = tm == 4
+    if short:
+        for n in range(1, tm):
+            greet(((z + n) % tm, j))
+    else:
+        @pl.when(z > 0)
+        def _():
+            greet((z - 1, j))
+
+        @pl.when(z < tm - 1)
+        def _():
+            greet((z + 1, j))
 
     if fused:
         greet((z, chip * 2 + 1 - core))
@@ -87,7 +92,7 @@
     pay[z, cout : cout + rows, :] = first.astype(BF16)
     pay[z, cout + rows :, :] = (second[:half] + half_roll(second[half:])).astype(BF16)
 
-    peers = jnp.where(z > 0, 1, 0) + jnp.where(z < tm - 1, 1, 0)
+    peers = tm - 1 if short else jnp.where(z > 0, 1, 0) + jnp.where(z < tm - 1, 1, 0)
     if fused:
         peers = peers + chips
     pl.semaphore_wait(barrier, peers)
@@ -118,10 +123,33 @@
         def _():
             to_left(step, z + step, h).start()
 
-    start_step(0, 0)
-    start_step(0, 1)
+    far, near, mirror = (z + 2) % 4, z + 1 - 2 * (z % 2), 3 - z
+    inner = (z == 1) | (z == 2)
+
+    def direct(n, shard, there):
+        return pltpu.make_async_remote_copy(
+            src_ref=pay.at[shard], dst_ref=pay.at[shard], send_sem=send_r.at[n, 0],
+            recv_sem=recv_r.at[n, 0], device_id=(there, j), device_id_type=MESH,
+        )
+
+    def relay():
+        return pltpu.make_async_remote_copy(
+            src_ref=pay.at[far], dst_ref=pay.at[far], send_sem=send_r.at[3, 0],
+            recv_sem=recv_r.at[2, 0], device_id=(near, j), device_id_type=MESH,
+        )
+
+    if short:
+        direct(0, z, far).start()
+        direct(1, z, near).start()
+    else:
+        start_step(0, 0)
+        start_step(0, 1)
 
     def each(start, stop, body):
+        for n in range(start, stop):
+            body(n)
+
+    def loop(start, stop, body):
         def step(n, unused):
             body(n)
             return unused
@@ -132,7 +160,7 @@
         def body(n):
             ref[n] = jnp.zeros(ref.shape[1:], BF16)
 
-        each(0, ref.shape[0], body)
+        loop(0, ref.shape[0], body)
 
     clear(ext)
     clear(cext)
@@ -206,7 +234,7 @@
             def _():
                 place(shard)
 
-        each(0, 2, side)
+        loop(0, 2, side)
         if step == 0:
             @pl.when(z + 1 <= tm - 1)
             def _():
@@ -254,18 +282,41 @@
             (((1,), (1,)), ((), ())), preferred_element_type=F32,
         )
 
+    def convolve():
+        each(0, 5, conv_four)
+        conv_ref[...] = conv_sum[...].astype(BF16)
+
     w_copy.wait()
     each(5, 7, conv_four)
-    pass_on(0, 0)
+    if not short:
+        pass_on(0, 0)
     each(6, 9, grad_three)
-    pass_on(0, 1)
-    lay_out(0)
-    each(0, 5, conv_four)
-    conv_ref[...] = conv_sum[...].astype(BF16)
-    for step in range(1, tm - 2):
-        pass_on(step, 0)
-        pass_on(step, 1)
-        lay_out(step)
+    if short:
+        direct(0, far, far).wait_recv()
+
+        @pl.when(inner)
+        def _():
+            relay().start()
+            direct(2, z, mirror).start()
+
+        direct(1, near, near).wait_recv()
+
+        def one(n):
+            place(jnp.where(n == 0, far, near))
+
+        loop(0, 2, one)
+
+        @pl.when(z % 2 == 0)
+        def _():
+            place_cot(next_tiles(), frames)
+    else:
+        pass_on(0, 1)
+        lay_out(0)
+        convolve()
+        for step in range(1, tm - 2):
+            pass_on(step, 0)
+            pass_on(step, 1)
+            lay_out(step)
 
     first_tap = z * slab // cin
 
@@ -291,33 +342,55 @@
         for r in range(1, chips):
             chip_copy(p, r).start()
 
-    def weight_part(p, cot_rows, at, count):
+    def weight_part(p, shards_of):
         one = first_tap + 2 * p
-        patches = jnp.concatenate(pair_tiles(split(one), split(one + 1), at, count), axis=1)
+        patches = jnp.concatenate(
+            [
+                jnp.concatenate(pair_tiles(split(one), split(one + 1), at * frames, count * frames), axis=1)
+                for at, count in shards_of
+            ],
+            axis=0,
+        )
+        cot_rows = jnp.concatenate(
+            [cot_t[at + n] for at, count in shards_of for n in range(count)], axis=1
+        )
         return jnp.dot(cot_rows, patches, preferred_element_type=F32).reshape(d32.shape[1:])
 
-    cot_all = jnp.concatenate([cot_t[s] for s in range(tm)], axis=1)
+    if short:
+        early_runs = [(jnp.where(z == 3, 2, 0), 1), (jnp.where(z < 2, 1, 3), 1)]
+        late_runs = [(jnp.where(z == 0, 2, 3 - z), 2)]
+    else:
+        early_runs = [(0, tm)]
+        late_runs = [(tm - 1 - z, 1)]
 
     def early(p):
-        d32[p] = weight_part(p, cot_all, 0, total)
+        d32[p] = weight_part(p, early_runs)
 
     each(0, pairs, early)
-    pass_on(tm - 2, 0)
-    pass_on(tm - 2, 1)
-    lay_out(tm - 2)
-    last = tm - 1 - z
+    if short:
+        @pl.when(z != 2)
+        def _():
+            convolve()
+
+        direct(2, mirror, mirror).wait_recv()
+        place(mirror)
+    else:
+        pass_on(tm - 2, 0)
+        pass_on(tm - 2, 1)
+        lay_out(tm - 2)
 
     def late(p):
-        @pl.when((z == 0) | (z == tm - 1))
-        def _():
-            d32[p] = d32[p] + weight_part(p, cot_t[last], last * frames, frames)
-
+        def add():
+            d32[p] = d32[p] + weight_part(p, late_runs)
+
+        if short:
+            add()
+        else:
+            pl.when((z == 0) | (z == tm - 1))(add)
         if fused:
             d16[p] = d32[p, 1 - core].astype(BF16)
             core_copy(p).start()
-
-            @pl.when(p > 0)
-            def _():
+            if p > 0:
                 core_sum(p - 1)
 
     each(0, pairs, late)
@@ -326,6 +399,15 @@
     else:
         for p in range(pairs):
             gw_ref[:, p * 2 * cin : (p + 1) * 2 * cin] = d32[p].reshape(cout, 2 * cin)
+    if short:
+        @pl.when(z == 1)
+        def _():
+            place_cot(next_tiles(), frames)
+
+        @pl.when(z == 2)
+        def _():
+            convolve()
+
     each(0, 6, grad_three)
     act_grad = grad_sum[...]
     d_normed = act_grad * (sig * (1.0 + normed * (1.0 - sig))) * gain
@@ -350,16 +432,25 @@
             for r in range(1, chips):
                 chip_copy(p, r).wait_send()
 
-    for step in range(tm - 1):
-        @pl.when((z < tm - 1) & (z - step >= 0))
-        def _():
-            for h in range(2):
-                to_right(step, z - step, h).wait_send()
-
-        @pl.when((z > 0) & (z + step <= tm - 1))
-        def _():
-            for h in range(2):
-                to_left(step, z + step, h).wait_send()
+    if short:
+        direct(0, z, far).wait_send()
+        direct(1, z, near).wait_send()
+
+        @pl.when(inner)
+        def _():
+            relay().wait_send()
+            direct(2, z, mirror).wait_send()
+    else:
+        for step in range(tm - 1):
+            @pl.when((z < tm - 1) & (z - step >= 0))
+            def _():
+                for h in range(2):
+                    to_right(step, z - step, h).wait_send()
+
+            @pl.when((z > 0) & (z + step <= tm - 1))
+            def _():
+                for h in range(2):
+                    to_left(step, z + step, h).wait_send()
 
 
 def emit(*refs):

time: 29.4 us -> 29.7 us (1.010)
  Pallas kernels: 28.6 us -> 28.9 us
    pallas_call x1, Pallas kernels: 27.8 us -> 28.1 us  [shards(): pl.pallas_call(functools.partial(kernel, cfg), out_shape=(jax.ShapeDtypeS...]
where the time goes in v6:
time: 29.7 us; the launch traced here: 29.5 us
  Pallas kernels  28.9 us (97%)
  between operations  0.64 us (2%)
    pallas_call x1, Pallas kernels, shards(): pl.pallas_call(functools.partial(kernel, cfg), out_shape=(jax.ShapeDtypeS...  28.1 us
    pallas_call x1, Pallas kernels, shards(): pl.pallas_call(emit, out_shape=tuple((jax.ShapeDtypeStruct(x.shape, x.dty...  0.79 us

profile of v6, /device:TPU:0, one launch (start us, length us, event | category | flops | bytes accessed | tf_op | source)
XLA Modules:
  0.0 29.5 jit_solution(3736090753176268956)
XLA Ops:
  0.6 28.1 %shard_map.76 = (bf16[128,384]{1,0:T(8,128)(2,1)S(1)}, bf16[128,192]{1,0:T(8,128)(2,1)S(1)}, f32[48,1296]{1,0:T(8,128)S(1)}) custom-call(bf16[128,192]{1,0:T(8,128)(2,1)} %bitcast.7, s32[1,8]{1,0:T(1,128)} %ids_ref.1, f32[1,192]{1,0:T(1,128)} %bitcast.8, bf16[5184,384]{1,0:T(8,128)(2,1)} %w_hbm.1, bf16[128,384]{1,0:T(8,128)(2,1)} %bitcast.6), custom_call_target="tpu_custom_call" | custom-call | tf_op jit(solution)/shard_map/pallas_call | solution.py:497
  28.7 0.8 %shard_map.77 = (bf16[128,384]{1,0:T(8,128)(2,1)}, bf16[128,192]{1,0:T(8,128)(2,1)}, f32[48,1296]{1,0:T(8,128)}) custom-call(bf16[128,384]{1,0:T(8,128)(2,1)S(1)} %get-tuple-element.9.refs_0_, bf16[128,192]{1,0:T(8,128)(2,1)S(1)} %get-tuple-element.10.refs_1_, f32[48,1296]{1,0:T(8,128)S(1)} %get-tuple-element.11.refs_2_), custom_call_target="tpu_custom_call" | custom-call | tf_op jit(solution)/shard_map/pallas_call | solution.py:540

commit v7 on v6

--- a/solution.py
+++ b/solution.py
@@ -372,6 +372,10 @@
         def _():
             convolve()
 
+        @pl.when(z != 1)
+        def _():
+            each(0, 4, grad_three)
+
         direct(2, mirror, mirror).wait_recv()
         place(mirror)
     else:
@@ -403,12 +407,13 @@
         @pl.when(z == 1)
         def _():
             place_cot(next_tiles(), frames)
+            each(0, 4, grad_three)
 
         @pl.when(z == 2)
         def _():
             convolve()
 
-    each(0, 6, grad_three)
+    each(4 if short else 0, 6, grad_three)
     act_grad = grad_sum[...]
     d_normed = act_grad * (sig * (1.0 + normed * (1.0 - sig))) * gain
     along = jnp.sum(d_normed * video, axis=1, keepdims=True) / cin

time: 29.7 us -> 29.6 us (level)
  no operation moved by 1% of the time
where the time goes in v7:
time: 29.6 us; the launch traced here: 29.5 us
  Pallas kernels  28.8 us (97%)
  between operations  0.64 us (2%)
    pallas_call x1, Pallas kernels, shards(): pl.pallas_call(functools.partial(kernel, cfg), out_shape=(jax.ShapeDtypeS...  28 us
    pallas_call x1, Pallas kernels, shards(): pl.pallas_call(emit, out_shape=tuple((jax.ShapeDtypeStruct(x.shape, x.dty...  0.79 us

profile of v7, /device:TPU:0, one launch (start us, length us, event | category | flops | bytes accessed | tf_op | source)
XLA Modules:
  0.0 29.5 jit_solution(1822122230452629568)
XLA Ops:
  0.6 28.0 %shard_map.76 = (bf16[128,384]{1,0:T(8,128)(2,1)S(1)}, bf16[128,192]{1,0:T(8,128)(2,1)S(1)}, f32[48,1296]{1,0:T(8,128)S(1)}) custom-call(bf16[128,192]{1,0:T(8,128)(2,1)} %bitcast.7, s32[1,8]{1,0:T(1,128)} %ids_ref.1, f32[1,192]{1,0:T(1,128)} %bitcast.8, bf16[5184,384]{1,0:T(8,128)(2,1)} %w_hbm.1, bf16[128,384]{1,0:T(8,128)(2,1)} %bitcast.6), custom_call_target="tpu_custom_call" | custom-call | tf_op jit(solution)/shard_map/pallas_call | solution.py:502
  28.7 0.8 %shard_map.77 = (bf16[128,384]{1,0:T(8,128)(2,1)}, bf16[128,192]{1,0:T(8,128)(2,1)}, f32[48,1296]{1,0:T(8,128)}) custom-call(bf16[128,384]{1,0:T(8,128)(2,1)S(1)} %get-tuple-element.9.refs_0_, bf16[128,192]{1,0:T(8,128)(2,1)S(1)} %get-tuple-element.10.refs_1_, f32[48,1296]{1,0:T(8,128)S(1)} %get-tuple-element.11.refs_2_), custom_call_target="tpu_custom_call" | custom-call | tf_op jit(solution)/shard_map/pallas_call | solution.py:545

commit v8 on v4

--- a/solution.py
+++ b/solution.py
@@ -275,10 +275,29 @@
             recv_sem=core_recv.at[p], device_id=(z, chip * 2 + 1 - core), device_id_type=MESH,
         )
 
-    def chip_copy(p, r):
+    skip = z * slab - first_tap * cin
+
+    def for_lanes(p, do):
+        if p == 0:
+            narrow, lanes = skip >= 128, (128, 2 * cin - 128)
+        elif p == pairs - 1:
+            narrow, lanes = skip + slab <= p * 2 * cin + 256, (0, 256)
+        else:
+            do((0, 2 * cin))
+            return
+
+        @pl.when(narrow)
+        def _():
+            do(lanes)
+
+        @pl.when(jnp.logical_not(narrow))
+        def _():
+            do((0, 2 * cin))
+
+    def chip_copy(p, r, lanes):
         there = (chip + r) % chips
         return pltpu.make_async_remote_copy(
-            src_ref=s16.at[p, there], dst_ref=r2.at[p, r - 1], send_sem=chip_send.at[p, r - 1],
+            src_ref=s16.at[p, there, :, pl.ds(*lanes)], dst_ref=r2.at[p, r - 1, :, pl.ds(*lanes)], send_sem=chip_send.at[p, r - 1],
             recv_sem=chip_recv.at[p, r - 1], device_id=(z, there * 2 + core), device_id_type=MESH,
         )
 
@@ -288,8 +307,7 @@
         both = both.reshape(chips, per, 2 * cin)
         s32[p] = both
         s16[p] = both.astype(BF16)
-        for r in range(1, chips):
-            chip_copy(p, r).start()
+        for_lanes(p, lambda lanes: [chip_copy(p, r, lanes).start() for r in range(1, chips)] and None)
 
     def weight_part(p, cot_rows, at, count):
         one = first_tap + 2 * p
@@ -333,18 +351,16 @@
         sums = []
         for p in range(pairs):
             own = s32[p, chip]
+            for_lanes(p, lambda lanes: [chip_copy(p, r, lanes).wait_recv() for r in range(1, chips)] and None)
             for r in range(1, chips):
-                chip_copy(p, r).wait_recv()
                 own = own + r2[p, r - 1].astype(F32)
             sums.append(own * scale)
         wide = jnp.concatenate(sums, axis=1)
-        skip = z * slab - first_tap * cin
         wide = pltpu.roll(wide, pairs * 2 * cin - skip, axis=1)
         gw_ref[...] = wide[:, :slab]
         for p in range(pairs):
             core_copy(p).wait_send()
-            for r in range(1, chips):
-                chip_copy(p, r).wait_send()
+            for_lanes(p, lambda lanes: [chip_copy(p, r, lanes).wait_send() for r in range(1, chips)] and None)
 
     for step in range(tm - 1):
         @pl.when((z < tm - 1) & (z - step >= 0))

time: 29.1 us -> 28.7 us (0.986)
  Pallas kernels: 28.3 us -> 27.9 us
    pallas_call x1, Pallas kernels: 27.5 us -> 27.2 us  [shards(): pl.pallas_call(functools.partial(kernel, cfg), out_shape=(jax.ShapeDtypeS...]
where the time goes in v8:
time: 28.7 us; the launch traced here: 28.6 us
  Pallas kernels  27.9 us (97%)
  between operations  0.64 us (2%)
    pallas_call x1, Pallas kernels, shards(): pl.pallas_call(functools.partial(kernel, cfg), out_shape=(jax.ShapeDtypeS...  27.2 us
    pallas_call x1, Pallas kernels, shards(): pl.pallas_call(emit, out_shape=tuple((jax.ShapeDtypeStruct(x.shape, x.dty...  0.79 us

profile of v8, /device:TPU:0, one launch (start us, length us, event | category | flops | bytes accessed | tf_op | source)
XLA Modules:
  0.0 28.6 jit_solution(16580966393859204850)
XLA Ops:
  0.6 27.2 %shard_map.76 = (bf16[128,384]{1,0:T(8,128)(2,1)S(1)}, bf16[128,192]{1,0:T(8,128)(2,1)S(1)}, f32[48,1296]{1,0:T(8,128)S(1)}) custom-call(bf16[128,192]{1,0:T(8,128)(2,1)} %bitcast.7, s32[1,8]{1,0:T(1,128)} %ids_ref.1, f32[1,192]{1,0:T(1,128)} %bitcast.8, bf16[5184,384]{1,0:T(8,128)(2,1)} %w_hbm.1, bf16[128,384]{1,0:T(8,128)(2,1)} %bitcast.6), custom_call_target="tpu_custom_call" | custom-call | tf_op jit(solution)/shard_map/pallas_call | solution.py:418
  27.8 0.8 %shard_map.77 = (bf16[128,384]{1,0:T(8,128)(2,1)}, bf16[128,192]{1,0:T(8,128)(2,1)}, f32[48,1296]{1,0:T(8,128)}) custom-call(bf16[128,384]{1,0:T(8,128)(2,1)S(1)} %get-tuple-element.9.refs_0_, bf16[128,192]{1,0:T(8,128)(2,1)S(1)} %get-tuple-element.10.refs_1_, f32[48,1296]{1,0:T(8,128)S(1)} %get-tuple-element.11.refs_2_), custom_call_target="tpu_custom_call" | custom-call | tf_op jit(solution)/shard_map/pallas_call | solution.py:459
